TPU v7x, 512 devices: a whole 4x4x16 slice. The times are simulated.
512 devices in a mesh: grp: 32 (over z, core), mem: 16 (over y, x).
Axes of the slice: x: 4, y: 4, z: 16, core: 2. Of those that a mesh axis runs over, the one named last changes fastest.
Arguments:
- amplitudes: bfloat16 [4096, 16384], P('grp', 'mem'), may hold values from -6 to 6
- amp_tiles: int32 [32, 128], P('grp', 'mem'), may hold values 0 or 1
- integrals: bfloat16 [16384, 4096], P('mem', 'grp'), may hold values from -0.046875 to 0.046875
- int_tiles: int32 [128, 32], P('mem', 'grp'), may hold values from 0 to 1, as said below
- denominators: float32 [4096, 4096], P('grp', 'mem'), may hold values from 0.5 to 4
Outputs:
- update: bfloat16 [4096, 4096], P('grp', 'mem')
Inputs may be any that keep to these rules, and one draw needn't show every extreme that they name: `int_tiles`: in each aligned block of 8 tile rows, every tile column holds exactly 6 ones.
All inputs are finite; a program needn't handle non-finite values. No bound on the sum of `amp_tiles` on one device may be relied on, other than what follows from the above.
Results may differ from a plain program's by a relative error of at most 0.001.
Values may be sent and summed in bfloat16 or wider, within the bound.
No kernel may reach another device: no remote copies, remote signals or barrier semaphores. Data moves between devices by JAX's collectives and lax.ppermute only.
A program may use at most 64 MiB of HBM per device.

v0:
```python
import jax
import jax.numpy as jnp
from jax import lax
from jax.sharding import PartitionSpec as P


def expand(mask, tile):
    return jnp.repeat(jnp.repeat(mask, tile, axis=0), tile, axis=1)


def on_device(amplitudes, amp_tiles, integrals, int_tiles, denominators):
    tile = amplitudes.shape[0] // amp_tiles.shape[0]
    masked_amp = amplitudes * expand(amp_tiles, tile).astype(jnp.bfloat16)
    masked_int = integrals * expand(int_tiles, tile).astype(jnp.bfloat16)
    partial_sum = jnp.dot(
        masked_amp,
        lax.all_gather(masked_int, "grp", axis=1, tiled=True),
        preferred_element_type=jnp.float32,
    )
    ladder = lax.psum_scatter(partial_sum, "mem", scatter_dimension=1, tiled=True)
    return (ladder / denominators).astype(jnp.bfloat16)


def solution(mesh):
    return jax.shard_map(
        on_device,
        mesh=mesh,
        in_specs=(
            P("grp", "mem"),
            P("grp", "mem"),
            P("mem", "grp"),
            P("mem", "grp"),
            P("grp", "mem"),
        ),
        out_specs=P("grp", "mem"),
        check_vma=False,
    )
```

profile of v0, /device:TPU:1, one launch (start us, length us, event | category | flops | bytes accessed | tf_op | source)
XLA Modules:
  0.0 210.0 jit_solution(6863702665777680717)
XLA Ops:
  6.5 0.0 all-gather.2.cloned.1.call-start
  6.5 0.7 convert_bitcast_fusion
  7.2 0.1 broadcast_bitcast_fusion
  7.3 1.9 broadcast_multiply_fusion
  9.1 0.0 all-gather.2.cloned.1.call-update
  9.2 0.0 reduce-scatter.2.cloned.1.call-start
  9.2 0.7 convert_bitcast_fusion.1
  9.9 0.1 broadcast_bitcast_fusion.1
  10.0 0.0 copy-start
  10.0 102.1 %all-gather.2.cloned.1.call-done = bf16[1024,4096]{1,0:T(8,128)(2,1)} async-done(((bf16[1024,128]{1,0:T(8,128)(2,1)}), bf16[1024,4096]{1,0:T(8,128)(2,1)}) %all-gather.2.cloned.1.call-update) | async-done | bytes 8388624 | tf_op jit(solution)/shard_map/all_gather | solution.py:17
  112.1 6.1 %fusion = f32[128,4096]{1,0:T(8,128)} fusion(bf16[1024,4096]{1,0:T(8,128)(2,1)} %all-gather.2.cloned.1.call-done, bf16[128,1024]{1,0:T(8,128)(2,1)} %param.5, bf16[1024]{0:T(1024)(128)(2,1)S(1)} %broadcast_bitcast_fusion.1), kind=kOutput, calls=%fused_computation | convolution fusion | flops 1073872896 | bytes 10749952 | tf_op jit(solution)/shard_map/dot_general | solution.py:15
  118.2 0.0 reduce-scatter.2.cloned.1.call-update
  118.2 83.4 %reduce-scatter.2.cloned.1.call-done = f32[128,256]{1,0:T(8,128)} async-done(((f32[128,4096]{1,0:T(8,128)}), f32[128,256]{1,0:T(8,128)}) %reduce-scatter.2.cloned.1.call-update) | async-done | bytes 131088 | tf_op jit(solution)/shard_map/reduce_scatter | solution.py:20
  201.6 0.0 copy-done
  201.6 1.6 divide_convert_fusion
Async XLA Ops:
  6.5 105.6 %all-gather.2.cloned.1.call-start = ((), (), s32[]{:S(2)}) async-start(), calls=%async_computation.1 | async-start | bytes 8650752 | tf_op jit(solution)/shard_map/all_gather | solution.py:17
  9.2 192.5 %reduce-scatter.2.cloned.1.call-start = ((), (), s32[]{:S(2)}) async-start(), calls=%async_computation.2 | async-start | bytes 2228224 | tf_op jit(solution)/shard_map/reduce_scatter | solution.py:20
  10.0 191.7 %copy-start = (f32[128,256]{1,0:T(8,128)S(1)}, f32[128,256]{1,0:T(8,128)}, u32[]{:S(2)}) copy-start(f32[128,256]{1,0:T(8,128)} %param.9) | copy-start | bytes 393220
Sparse Core Ops, SparseCore 0:
  9.4 102.6 all-gather.1
  118.3 83.2 reduce-scatter.1
where the time goes:
time: 211 us; the launch traced here: 210 us
  waiting for transfers between devices  186 us (88%)
  between operations  13.4 us (6%)
  matrix products  6.1 us (3%)
  other arithmetic  4.75 us (2%)
    all_gather x1, waiting for transfers between devices, on_device(): lax.all_gather(masked_int, 'grp', axis=1, tiled=True)  102 us
    reduce_scatter x1, waiting for transfers between devices, on_device(): lax.psum_scatter(partial_sum, 'mem', scatter_dimension=1, tiled=True)  83.4 us
    dot_general x1, matrix products, on_device(): jnp.dot(masked_amp, lax.all_gather(masked_int, 'grp', axis=1, tiled=True)...  6.1 us
  transfers between devices with their start and end apart: 2, of which 2 were waited for; matrix products, arithmetic and copies ran while one was open for 0% of the time, Pallas kernels for 0%

commit v1 on v0

v1 whole, which is shorter than its diff:
```python
import jax
import jax.numpy as jnp
from jax import lax
from jax.sharding import PartitionSpec as P

NZ = 6
ROW = 16


def pick(options, which):
    out = options[-1]
    for at in range(len(options) - 2, -1, -1):
        out = jnp.where(which == at, options[at], out)
    return out


def pack(integrals, int_tiles, tile):
    kt = int_tiles.shape[0]
    blocks = integrals.reshape(kt, tile, tile)
    zeros = jnp.cumsum(1 - int_tiles[:, 0])
    slots = []
    for i in range(NZ):
        lag = sum((zeros[i + o] > o).astype(jnp.int32) for o in range(kt - NZ))
        slots.append(pick([blocks[i + o] for o in range(kt - NZ + 1)], lag))
    slots = jnp.stack(slots).astype(jnp.float32)
    top = jnp.max(jnp.abs(slots), axis=1)
    shift = jnp.clip(jnp.floor(14.0 - jnp.log2(jnp.maximum(top, 1e-37))), 0.0, 120.0)
    values = (slots * jnp.exp2(shift)[:, None, :]).astype(jnp.float16)
    mask = jnp.broadcast_to(int_tiles.astype(jnp.float32), (kt, tile))
    note = jnp.concatenate([shift, mask, jnp.zeros((ROW - NZ - kt, tile), jnp.float32)])
    return jnp.concatenate([values.reshape(NZ * tile, tile), note.astype(jnp.float16)])


def unpack(packed, kt, tile):
    groups = packed.shape[0]
    values = packed[:, : NZ * tile].reshape(groups, NZ, tile, tile).astype(jnp.float32)
    note = packed[:, NZ * tile :].astype(jnp.float32)
    shift, mask = note[:, :NZ], note[:, NZ : NZ + kt]
    slots = (values * jnp.exp2(-shift)[:, :, None, :]).astype(jnp.bfloat16)
    zeros = jnp.cumsum(1.0 - mask, axis=1)
    full = []
    for k in range(kt):
        out = jnp.zeros_like(slots[:, 0])
        for o in range(kt - NZ + 1):
            if 0 <= k - o < NZ:
                here = (mask[:, k] > 0) & (zeros[:, k] == o)
                out = jnp.where(here[:, None, :], slots[:, k - o], out)
        full.append(out)
    return jnp.concatenate(full, axis=1)


def on_device(amplitudes, amp_tiles, integrals, int_tiles, denominators):
    rows, depth = amplitudes.shape
    kt = int_tiles.shape[0]
    tile = depth // kt
    owners, width = lax.axis_size("mem"), denominators.shape[1]
    masked_amp = amplitudes * jnp.repeat(amp_tiles, tile, axis=1).astype(jnp.bfloat16)
    everyone = lax.all_gather(pack(integrals, int_tiles, tile), "grp")
    masked_int = unpack(everyone, kt, tile)
    masked_int = masked_int.reshape(owners, -1, depth, tile)
    partial_sum = jnp.einsum(
        "rk,obkc->orbc", masked_amp, masked_int, preferred_element_type=jnp.float32
    ).reshape(owners, rows, width)
    ladder = jnp.sum(lax.all_to_all(partial_sum, "mem", 0, 0), axis=0)
    return (ladder / denominators).astype(jnp.bfloat16)


def solution(mesh):
    return jax.shard_map(
        on_device,
        mesh=mesh,
        in_specs=(
            P("grp", "mem"),
            P("grp", "mem"),
            P("mem", "grp"),
            P("mem", "grp"),
            P("grp", "mem"),
        ),
        out_specs=P("grp", "mem"),
        check_vma=False,
    )
```

time: 211 us -> 165 us (0.78)
  waiting for transfers between devices: 186 us -> 32.8 us
  blocking collectives: 0 us -> 60.4 us
  other arithmetic: 4.75 us -> 33.1 us
  local copies, waits for them, and re-layouts: 0.15 us -> 19 us
  starting transfers between devices: 0.04 us -> 6.76 us
  between operations: 13.4 us -> 7.99 us
  matrix products: 6.1 us -> 3.78 us
    all_gather x1 -> x0, waiting for transfers between devices: 102 us -> none  [on_device(): lax.all_gather(masked_int, 'grp', axis=1, tiled=True)]
    reduce_scatter x1 -> x0, waiting for transfers between devices: 83.4 us -> none  [on_device(): lax.psum_scatter(partial_sum, 'mem', scatter_dimension=1, tiled=True)]
    all_gather x0 -> x1, blocking collectives: none -> 60.4 us  [on_device(): everyone = lax.all_gather(pack(integrals, int_tiles, tile), 'grp')]
    all_to_all x0 -> x1, waiting for transfers between devices: none -> 32.8 us  [on_device(): ladder = jnp.sum(lax.all_to_all(partial_sum, 'mem', 0, 0), axis=0)]
    unnamed x0 -> x12, other arithmetic: none -> 23.9 us
    slice x0 -> x9, local copies, waits for them, and re-layouts: none -> 17.6 us  [the longest x7 12.6 us: unpack(): out = jnp.where(here[:, None, :], slots[:, k - o], out)]
    all_to_all x0 -> x1, starting transfers between devices: none -> 6.76 us  [on_device(): ladder = jnp.sum(lax.all_to_all(partial_sum, 'mem', 0, 0), axis=0)]
    convert_element_type x2 -> x4, other arithmetic: 1.32 us -> 4.7 us  [the longest x1 4.62 us: unpack(): slots = (values * jnp.exp2(-shift)[:, :, None, :]).astype(jnp.bfloat16)]
  transfers between devices with their start and end apart: 2 -> 1, of which waited for: 2 -> 1; matrix products, arithmetic and copies ran while one was open for 0% -> 0% of each run, Pallas kernels for 0% -> 0%
where the time goes in v1:
time: 165 us; the launch traced here: 164 us
  blocking collectives  60.4 us (37%)
  other arithmetic  33.1 us (20%)
  waiting for transfers between devices  32.8 us (20%)
  local copies, waits for them, and re-layouts  19 us (12%)
  between operations  7.99 us (5%)
  starting transfers between devices  6.76 us (4%)
  matrix products  3.78 us (2%)
    all_gather x1, blocking collectives, on_device(): everyone = lax.all_gather(pack(integrals, int_tiles, tile), 'grp')  60.4 us
    all_to_all x1, waiting for transfers between devices, on_device(): ladder = jnp.sum(lax.all_to_all(partial_sum, 'mem', 0, 0), axis=0)  32.8 us
    unnamed x12, other arithmetic  23.9 us
    slice x7, local copies, waits for them, and re-layouts, unpack(): out = jnp.where(here[:, None, :], slots[:, k - o], out)  12.6 us
    all_to_all x1, starting transfers between devices, on_device(): ladder = jnp.sum(lax.all_to_all(partial_sum, 'mem', 0, 0), axis=0)  6.76 us
    convert_element_type x1, other arithmetic, unpack(): slots = (values * jnp.exp2(-shift)[:, :, None, :]).astype(jnp.bfloat16)  4.62 us
    slice x1, local copies, waits for them, and re-layouts, unpack(): packed[:, :NZ * tile].reshape(groups, NZ, tile, tile).astype(jnp.float32)  4.33 us
    dot_general x1, matrix products, on_device(): jnp.einsum('rk,obkc->orbc', masked_amp, masked_int, preferred_element_typ...  3.78 us
  transfers between devices with their start and end apart: 1, of which 1 were waited for; matrix products, arithmetic and copies ran while one was open for 0% of the time, Pallas kernels for 0%

profile of v1, /device:TPU:1, one launch (start us, length us, event | category | flops | bytes accessed | tf_op | source)
XLA Modules:
  0.0 163.8 jit_solution(951551737173352767)
XLA Ops:
  0.0 0.7 convert_bitcast_fusion
  0.7 0.2 reduce-window.4
  0.9 0.7 fusion.11
  9.2 0.1 pad.2.clone
  9.3 0.1 pad.3.clone
  9.4 0.8 bitcast_dynamic-update-slice_fusion.5
  10.2 0.8 bitcast_dynamic-update-slice_fusion.4
  11.0 0.8 bitcast_dynamic-update-slice_fusion.3
  11.9 0.8 bitcast_dynamic-update-slice_fusion.2
  12.7 0.8 bitcast_dynamic-update-slice_fusion.1
  13.5 0.8 bitcast_dynamic-update-slice_fusion
  14.4 0.1 fusion.2
  14.4 0.3 maximum_maximum_fusion
  14.7 60.4 %all-gather.2 = f16[25088,128]{1,0:T(8,128)(2,1)S(1)} all-gather(f16[784,128]{1,0:T(8,128)(2,1)S(1)} %maximum_maximum_fusion), channel_id=2, replica_groups=mesh['grp'=32,'mem'=16] {'grp'}, dimensions={0}, use_global_device_ids=true | all-gather | bytes 6623232 | tf_op jit(solution)/shard_map/all_gather | solution.py:58
  75.1 0.0 copy-start.5
  75.2 4.3 %slice.238 = f16[32,768,128]{2,1,0:T(8,128)(2,1)} slice(f16[32,784,128]{2,1,0:T(8,128)(2,1)S(1)} %bitcast.50), slice={[0:32], [0:768], [0:128]} | slice | bytes 12582912 | tf_op jit(solution)/shard_map/slice | solution.py:36
  79.6 0.1 reduce_window_sum.18
  79.7 0.6 and_reduce_fusion
  80.3 0.6 and_reduce_fusion.2
  80.9 0.0 copy-done.5
  80.9 0.1 broadcast_bitcast_fusion
  81.0 4.6 %fusion = bf16[32,6,128,128]{3,2,1,0:T(8,128)(2,1)S(1)} fusion(f16[32,6,128,128]{3,2,1,0:T(8,128)(2,1)} %bitcast.51, f32[32,6,128]{2,1,0:T(8,128)S(1)} %fusion.7), kind=kLoop, calls=%fused_computation.1 | loop fusion | flops 9437184 | bytes 12681216 | tf_op jit(solution)/shard_map/convert_element_type | solution.py:39
  85.6 2.8 %fusion.10 = (bf16[32,1,128,128]{3,2,1,0:T(8,128)(2,1)S(1)}, bf16[32,1,128,128]{3,2,1,0:T(8,128)(2,1)}, bf16[32,1,128,128]{3,2,1,0:T(8,128)(2,1)}, bf16[32,1,128...) fusion(bf16[32,6,128,128]{3,2,1,0:T(8,128)(2,1)S(1)} %fusion), kind=kLoop, calls=%fused_computation.60 | loop fusion | bytes 12582912 | tf_op jit(solution)/shard_map/slice | solution.py:47
  88.4 0.7 copy.18
  89.4 1.6 copy.17
  91.0 2.3 %copy.16 = bf16[32,1,128,128]{2,3,0,1:T(8,128)(2,1)} copy(bf16[32,1,128,128]{3,2,1,0:T(8,128)(2,1)} %get-tuple-element.25) | data formatting | bytes 2097152 | tf_op jit(solution)/shard_map/slice | solution.py:47
  93.3 2.3 %copy.15 = bf16[32,1,128,128]{2,3,0,1:T(8,128)(2,1)} copy(bf16[32,1,128,128]{3,2,1,0:T(8,128)(2,1)} %get-tuple-element.26) | data formatting | bytes 2097152 | tf_op jit(solution)/shard_map/slice | solution.py:47
  95.6 1.3 copy.14
  96.9 1.6 copy.13
  98.6 0.0 copy-start
  98.6 0.0 copy-start.1
  98.6 0.0 copy-start.2
  98.6 0.7 select_dynamic-update-slice_fusion.7
  99.3 3.5 %select_dynamic-update-slice_fusion.6 = bf16[16,2,1024,128]{2,3,1,0:T(8,128)(2,1)S(1)} fusion(bf16[16,2,1024,128]{2,3,1,0:T(8,128)(2,1)S(1)} %select_dynamic-update-slice_fusion.7, bf16[16,2,128,128]{2,3,1,0:T(8,128)(2,1)S(1)} %bitcast.56, bf16[16,2,128,128]{2,3,1,0:T(8,128)(2,1)} %bitcast.61, pred[16,2,128]{2,1,0:T(4,128)(4,1)S(1)} %broadcast_in_dim.169, ...), kind=kLoop, calls=%fused_computation.8 | loop fusion | flops 1048576 | bytes 3162112
  102.8 5.7 %select_dynamic-update-slice_fusion.5 = bf16[16,2,1024,128]{2,3,1,0:T(8,128)(2,1)S(1)} fusion(bf16[16,2,1024,128]{2,3,1,0:T(8,128)(2,1)S(1)} %select_dynamic-update-slice_fusion.6, bf16[16,2,128,128]{2,3,1,0:T(8,128)(2,1)S(1)} %bitcast.57, bf16[16,2,128,128]{2,3,1,0:T(8,128)(2,1)} %bitcast.62, bf16[16,2,128,128]{2,3,1,0:T(8,128)(2,1)} %bitcast.67, ...), kind=kLoop, calls=%fused_computation.7 | loop fusion | flops 1572864 | bytes 4218880
  108.4 0.0 copy-done
  108.5 0.0 copy-done.1
  108.5 0.0 copy-done.2
  108.5 0.0 copy-start.3
  108.5 2.7 %select_dynamic-update-slice_fusion.4 = bf16[16,2,1024,128]{2,3,1,0:T(8,128)(2,1)S(1)} fusion(bf16[16,2,1024,128]{2,3,1,0:T(8,128)(2,1)S(1)} %select_dynamic-update-slice_fusion.5, bf16[16,2,128,128]{2,3,1,0:T(8,128)(2,1)S(1)} %bitcast.63, bf16[16,2,128,128]{2,3,1,0:T(8,128)(2,1)S(1)} %bitcast.68, bf16[16,2,128,128]{2,3,1,0:T(8,128)(2,1)S(1)} %bitcast.64, ...), kind=kLoop, calls=%fused_computation.6 | loop fusion | flops 1572864 | bytes 4218880
  111.2 2.7 %select_dynamic-update-slice_fusion.3 = bf16[16,2,1024,128]{2,3,1,0:T(8,128)(2,1)S(1)} fusion(bf16[16,2,1024,128]{2,3,1,0:T(8,128)(2,1)S(1)} %select_dynamic-update-slice_fusion.4, bf16[16,2,128,128]{2,3,1,0:T(8,128)(2,1)S(1)} %bitcast.69, bf16[16,2,128,128]{2,3,1,0:T(8,128)(2,1)S(1)} %bitcast.65, bf16[16,2,128,128]{2,3,1,0:T(8,128)(2,1)S(1)} %bitcast.58, ...), kind=kLoop, calls=%fused_computation.5 | loop fusion | flops 1572864 | bytes 4218880
  114.0 2.7 %select_dynamic-update-slice_fusion.2 = bf16[16,2,1024,128]{2,3,1,0:T(8,128)(2,1)S(1)} fusion(bf16[16,2,1024,128]{2,3,1,0:T(8,128)(2,1)S(1)} %select_dynamic-update-slice_fusion.3, bf16[16,2,128,128]{2,3,1,0:T(8,128)(2,1)S(1)} %bitcast.66, bf16[16,2,128,128]{2,3,1,0:T(8,128)(2,1)S(1)} %bitcast.59, bf16[16,2,128,128]{2,3,1,0:T(8,128)(2,1)S(1)} %bitcast.52, ...), kind=kLoop, calls=%fused_computation.4 | loop fusion | flops 1572864 | bytes 4218880
  116.7 1.8 %select_dynamic-update-slice_fusion.1 = bf16[16,2,1024,128]{2,3,1,0:T(8,128)(2,1)S(1)} fusion(bf16[16,2,1024,128]{2,3,1,0:T(8,128)(2,1)S(1)} %select_dynamic-update-slice_fusion.2, bf16[16,2,128,128]{2,3,1,0:T(8,128)(2,1)S(1)} %bitcast.60, bf16[16,2,128,128]{2,3,1,0:T(8,128)(2,1)S(1)} %bitcast.53, pred[16,2,128]{2,1,0:T(4,128)(4,1)S(1)} %broadcast_in_dim.197, ...), kind=kLoop, calls=%fused_computation.3 | loop fusion | flops 1048576 | bytes 3162112
  118.5 1.0 select_dynamic-update-slice_fusion
  119.5 0.0 copy-done.3
  119.5 0.0 copy-start.4
  119.5 3.8 %fusion.3 = f32[16,2,128,128]{3,2,1,0:T(8,128)} fusion(bf16[16,2,1024,128]{2,3,1,0:T(8,128)(2,1)S(1)} %select_dynamic-update-slice_fusion, bf16[128,1024]{1,0:T(8,128)(2,1)S(1)} %copy-done.3, bf16[1024]{0:T(1024)(128)(2,1)S(1)} %broadcast_bitcast_fusion), kind=kOutput, calls=%fused_computation.14 | convolution fusion | flops 1073872896 | bytes 10749952 | tf_op jit(solution)/shard_map/rk,obkc->orbc/dot_general | solution.py:61
  123.3 6.8 %all-to-all-start = ((f32[16,128,256]{1,2,0:T(8,128)}), f32[16,128,256]{1,2,0:T(8,128)S(1)}, u32[]{:S(2)}, u32[]{:S(2)}) async-start(f32[16,128,256]{1,2,0:T(8,128)} %bitcast.33), calls=%async_computation | async-start | bytes 4194304 | tf_op jit(solution)/shard_map/all_to_all | solution.py:64
  130.0 0.0 copy-done.4
  130.0 0.1 copy.19
  130.1 32.8 %all-to-all-done = f32[16,128,256]{1,2,0:T(8,128)S(1)} async-done(((f32[16,128,256]{1,2,0:T(8,128)}), f32[16,128,256]{1,2,0:T(8,128)S(1)}, u32[]{:S(2)}, u32[]{:S(2)}) %all-to-all-start) | async-done | bytes 2097184 | tf_op jit(solution)/shard_map/all_to_all | solution.py:64
  162.9 0.1 reduce_sum.9
  163.1 0.7 copy.20
  (26 shorter events, 0.4 us)
Async XLA Ops:
  75.1 5.7 %copy-start.5 = (s32[1,8]{1,0:T(1,128)S(1)}, s32[1,8]{1,0:T(1,128)}, u32[]{:S(2)}) copy-start(s32[1,8]{1,0:T(1,128)} %param.6) | copy-start | bytes 100
  98.6 9.9 %copy-start = (bf16[32,1,128,128]{2,3,0,1:T(8,128)(2,1)S(1)}, bf16[32,1,128,128]{2,3,0,1:T(8,128)(2,1)}, u32[]{:S(2)}) copy-start(bf16[32,1,128,128]{2,3,0,1:T(8,128)(2,1)} %copy.14) | copy-start | bytes 3145732
  98.6 9.9 %copy-start.1 = (bf16[32,1,128,128]{2,3,0,1:T(8,128)(2,1)S(1)}, bf16[32,1,128,128]{2,3,0,1:T(8,128)(2,1)}, u32[]{:S(2)}) copy-start(bf16[32,1,128,128]{2,3,0,1:T(8,128)(2,1)} %copy.16) | copy-start | bytes 3145732
  98.6 9.9 %copy-start.2 = (bf16[32,1,128,128]{2,3,0,1:T(8,128)(2,1)S(1)}, bf16[32,1,128,128]{2,3,0,1:T(8,128)(2,1)}, u32[]{:S(2)}) copy-start(bf16[32,1,128,128]{2,3,0,1:T(8,128)(2,1)} %copy.15) | copy-start | bytes 3145732
  108.5 11.0 %copy-start.3 = (bf16[128,1024]{1,0:T(8,128)(2,1)S(1)}, bf16[128,1024]{1,0:T(8,128)(2,1)}, u32[]{:S(2)}) copy-start(bf16[128,1024]{1,0:T(8,128)(2,1)} %param.5) | copy-start | bytes 786436
  119.5 10.6 %copy-start.4 = (f32[128,256]{1,0:T(8,128)S(1)}, f32[128,256]{1,0:T(8,128)}, u32[]{:S(2)}) copy-start(f32[128,256]{1,0:T(8,128)} %param.9) | copy-start | bytes 393220
  123.3 39.7 %all-to-all-start = ((f32[16,128,256]{1,2,0:T(8,128)}), f32[16,128,256]{1,2,0:T(8,128)S(1)}, u32[]{:S(2)}, u32[]{:S(2)}) async-start(f32[16,128,256]{1,2,0:T(8,128)} %bitcast.33), calls=%async_computation | async-start | bytes 4194304 | tf_op jit(solution)/shard_map/all_to_all | solution.py:64

commit v2 on v0

v2 whole, which is shorter than its diff:
```python
import functools

import jax
import jax.numpy as jnp
from jax import lax
from jax.experimental import pallas as pl
from jax.experimental.pallas import tpu as pltpu
from jax.sharding import PartitionSpec as P

NZ = 6
NOTE = 16
FINE = 8.0
VMEM = pl.BlockSpec(memory_space=pltpu.VMEM)
SMEM = pl.BlockSpec(memory_space=pltpu.SMEM)


def to_int16(values):
    return jnp.round(values).astype(jnp.int32).astype(jnp.int16)


def note_of(rows, width):
    at = lax.broadcasted_iota(jnp.int32, (NOTE, width), 0)
    note = jnp.zeros((NOTE, width), jnp.float32)
    for i, row in enumerate(rows):
        note = jnp.where(at == i, row, note)
    return to_int16(note)


def pack_kernel(kt, tile, tiles_ref, integrals_ref, out_ref):
    ones = [tiles_ref[k, 0] for k in range(kt)]
    zeros = [sum(1 - ones[j] for j in range(k + 1)) for k in range(kt)]
    shifts = []
    for i in range(NZ):
        at = i
        for o in range(kt - NZ):
            at = at + (zeros[i + o] > o).astype(jnp.int32)
        start = pl.multiple_of(at * tile, tile)
        block = integrals_ref[pl.ds(start, tile), :].astype(jnp.float32)
        top = jnp.max(jnp.abs(block), axis=0, keepdims=True)
        shift = jnp.floor(14.99 - jnp.log2(jnp.maximum(top, 1e-37)))
        shift = jnp.clip(shift, 0.0, 120.0)
        out_ref[i * tile : (i + 1) * tile] = to_int16(block * jnp.exp2(shift))
        shifts.append(shift)
    mask = [one.astype(jnp.float32) for one in ones]
    out_ref[NZ * tile :] = note_of(shifts + mask, tile)


def ladder_kernel(kt, tile, tiles_ref, amp_ref, packed_ref, out_ref, masked, full):
    groups = out_ref.shape[0]
    per = packed_ref.shape[0] // groups
    rows = amp_ref.shape[0]

    @pl.when(pl.program_id(0) == 0)
    def _():
        for k in range(kt):
            cols = slice(k * tile, (k + 1) * tile)
            keep = tiles_ref[0, k].astype(jnp.float32)
            masked[:, cols] = (amp_ref[:, cols].astype(jnp.float32) * keep).astype(
                jnp.bfloat16
            )

    for g in range(groups):
        for j in range(per):
            b = g * per + j
            note = packed_ref[b, NZ * tile :].astype(jnp.int32).astype(jnp.float32)
            slots = []
            for i in range(NZ):
                block = packed_ref[b, i * tile : (i + 1) * tile]
                block = block.astype(jnp.int32).astype(jnp.float32)
                slots.append((block * jnp.exp2(-note[i : i + 1])).astype(jnp.bfloat16))
            zeros = jnp.zeros((1, tile), jnp.float32)
            for k in range(kt):
                one = note[NZ + k : NZ + k + 1]
                zeros = zeros + (1.0 - one)
                out = None
                for o in range(kt - NZ + 1):
                    if 0 <= k - o < NZ:
                        here = jnp.where(zeros == o, one, 0.0).astype(jnp.bfloat16)
                        term = slots[k - o] * here
                        out = term if out is None else out + term
                full[g, k * tile : (k + 1) * tile, j * tile : (j + 1) * tile] = out
        part = jnp.dot(masked[...], full[g], preferred_element_type=jnp.float32)
        top = jnp.max(jnp.abs(part), axis=0, keepdims=True)
        shift = jnp.floor(FINE * (14.999 - jnp.log2(jnp.maximum(top, 1e-30))))
        out_ref[g, :rows] = to_int16(part * jnp.exp2(shift / FINE))
        out_ref[g, rows:] = note_of([shift], part.shape[1])


def update_kernel(parts_ref, denominators_ref, out_ref):
    rows = denominators_ref.shape[0]
    total = jnp.zeros(denominators_ref.shape, jnp.float32)
    for i in range(parts_ref.shape[0]):
        note = parts_ref[i, rows:].astype(jnp.int32).astype(jnp.float32)
        part = parts_ref[i, :rows].astype(jnp.int32).astype(jnp.float32)
        total = total + part * jnp.exp2(note[:1] / -FINE)
    out_ref[...] = (total / denominators_ref[...]).astype(out_ref.dtype)


def on_device(amplitudes, amp_tiles, integrals, int_tiles, denominators):
    rows, depth = amplitudes.shape
    kt = int_tiles.shape[0]
    tile = depth // kt
    owners, width = lax.axis_size("mem"), denominators.shape[1]
    packed = pl.pallas_call(
        functools.partial(pack_kernel, kt, tile),
        out_shape=jax.ShapeDtypeStruct((NZ * tile + NOTE, tile), jnp.int16),
        in_specs=[SMEM, VMEM],
        out_specs=VMEM,
        name="pack",
    )(int_tiles, integrals)
    everyone = lax.all_gather(packed, "grp")
    per = width // tile
    step = 2
    parts = pl.pallas_call(
        functools.partial(ladder_kernel, kt, tile),
        out_shape=jax.ShapeDtypeStruct((owners, rows + NOTE, width), jnp.int16),
        grid=(owners // step,),
        in_specs=[
            SMEM,
            pl.BlockSpec((rows, depth), lambda s: (0, 0)),
            pl.BlockSpec((step * per, NZ * tile + NOTE, tile), lambda s: (s, 0, 0)),
        ],
        out_specs=pl.BlockSpec((step, rows + NOTE, width), lambda s: (s, 0, 0)),
        scratch_shapes=[
            pltpu.VMEM((rows, depth), jnp.bfloat16),
            pltpu.VMEM((step, depth, width), jnp.bfloat16),
        ],
        compiler_params=pltpu.CompilerParams(vmem_limit_bytes=32 * 2**20),
        name="ladder",
    )(amp_tiles, amplitudes, everyone)
    return pl.pallas_call(
        update_kernel,
        out_shape=jax.ShapeDtypeStruct((rows, width), jnp.bfloat16),
        in_specs=[VMEM, VMEM],
        out_specs=VMEM,
        name="update",
    )(lax.all_to_all(parts, "mem", 0, 0), denominators)


def solution(mesh):
    return jax.shard_map(
        on_device,
        mesh=mesh,
        in_specs=(
            P("grp", "mem"),
            P("grp", "mem"),
            P("mem", "grp"),
            P("mem", "grp"),
            P("grp", "mem"),
        ),
        out_specs=P("grp", "mem"),
        check_vma=False,
    )
```

time: 211 us -> 98.4 us (0.47)
  waiting for transfers between devices: 186 us -> 0 us
  blocking collectives: 0 us -> 85.8 us
  between operations: 13.4 us -> 0.01 us
  Pallas kernels: 0 us -> 11.1 us
  matrix products: 6.1 us -> 0 us
  other arithmetic: 4.75 us -> 0 us
    all_gather x1 -> x0, waiting for transfers between devices: 102 us -> none  [on_device(): lax.all_gather(masked_int, 'grp', axis=1, tiled=True)]
    reduce_scatter x1 -> x0, waiting for transfers between devices: 83.4 us -> none  [on_device(): lax.psum_scatter(partial_sum, 'mem', scatter_dimension=1, tiled=True)]
    all_gather x0 -> x1, blocking collectives: none -> 60.8 us  [on_device(): everyone = lax.all_gather(packed, 'grp')]
    all_to_all x0 -> x1, blocking collectives: none -> 24.9 us  [on_device(): lax.all_to_all(parts, 'mem', 0, 0)]
    pallas_call x0 -> x3, Pallas kernels: none -> 11.1 us  [the longest x1 7.14 us: on_device(): pl.pallas_call(functools.partial(ladder_kernel, kt, tile), out_shape=jax....]
    dot_general x1 -> x0, matrix products: 6.1 us -> none  [on_device(): jnp.dot(masked_amp, lax.all_gather(masked_int, 'grp', axis=1, tiled=True)...]
    convert_element_type x3 -> x0, other arithmetic: 2.88 us -> none  [the longest x1 1.56 us: on_device(): return (ladder / denominators).astype(jnp.bfloat16)]
  transfers between devices with their start and end apart: 2 -> 0, of which waited for: 2 -> 0; matrix products, arithmetic and copies ran while one was open for 0% -> 0% of each run, Pallas kernels for 0% -> 0%
where the time goes in v2:
time: 98.4 us; the launch traced here: 98.2 us
  blocking collectives  85.8 us (87%)
  Pallas kernels  11.1 us (11%)
  local copies, waits for them, and re-layouts  1.33 us (1%)
    all_gather x1, blocking collectives, on_device(): everyone = lax.all_gather(packed, 'grp')  60.8 us
    all_to_all x1, blocking collectives, on_device(): lax.all_to_all(parts, 'mem', 0, 0)  24.9 us
    pallas_call x1, Pallas kernels, on_device(): pl.pallas_call(functools.partial(ladder_kernel, kt, tile), out_shape=jax....  7.14 us
    pallas_call x1, Pallas kernels, on_device(): pl.pallas_call(update_kernel, out_shape=jax.ShapeDtypeStruct((rows, width...  2.21 us

profile of v2, /device:TPU:1, one launch (start us, length us, event | category | flops | bytes accessed | tf_op | source)
XLA Modules:
  0.0 98.2 jit_solution(1213225324231903436)
XLA Ops:
  0.0 1.3 %copy.6.tiles_ref = s32[8,1]{1,0:T(8,128)} copy(s32[8,1]{0,1:T(1,128)} %param.8) | data formatting | bytes 64 | tf_op args[3]
  1.3 1.7 %pack.1 = s16[784,128]{1,0:T(8,128)(2,1)} custom-call(s32[8,1]{1,0:T(8,128)} %copy.6.tiles_ref, bf16[1024,128]{1,0:T(8,128)(2,1)} %integrals_ref.1), custom_call_target="tpu_custom_call" | custom-call | tf_op jit(solution)/shard_map/pack/pallas_call | solution.py:104
  3.1 0.0 copy-start
  3.1 0.0 copy-start.1
  3.1 60.8 %all-gather.2 = s16[25088,128]{1,0:T(8,128)(2,1)S(1)} all-gather(s16[784,128]{1,0:T(8,128)(2,1)} %pack.1), channel_id=2, replica_groups=mesh['grp'=32,'mem'=16] {'grp'}, dimensions={0}, use_global_device_ids=true | all-gather | bytes 6623232 | tf_op jit(solution)/shard_map/all_gather | solution.py:111
  63.9 0.0 copy-done
  63.9 0.0 copy-done.1
  63.9 7.1 %ladder.1 = s16[16,144,256]{2,1,0:T(8,128)(2,1)S(1)} custom-call(s32[1,8]{1,0:T(1,128)S(1)} %copy-done.1, bf16[128,1024]{1,0:T(8,128)(2,1)S(1)} %copy-done, s16[32,784,128]{2,1,0:T(8,128)(2,1)S(1)} %bitcast.1), custom_call_target="tpu_custom_call" | custom-call | tf_op jit(solution)/shard_map/ladder/pallas_call | solution.py:114
  71.0 24.9 %all_to_all.5.parts_ref = s16[16,144,256]{2,1,0:T(8,128)(2,1)} all-to-all(s16[16,144,256]{2,1,0:T(8,128)(2,1)S(1)} %ladder.1), channel_id=1, replica_groups=mesh['grp'=32,'mem'=16] {'mem'}, dimensions={0} | all-to-all | bytes 2359296 | tf_op jit(solution)/shard_map/all_to_all | solution.py:137
  96.0 2.2 %update.1 = bf16[128,256]{1,0:T(8,128)(2,1)} custom-call(s16[16,144,256]{2,1,0:T(8,128)(2,1)} %all_to_all.5.parts_ref, f32[128,256]{1,0:T(8,128)} %denominators_ref.1), custom_call_target="tpu_custom_call" | custom-call | tf_op jit(solution)/shard_map/update/pallas_call | solution.py:131
Async XLA Ops:
  3.1 60.8 %copy-start = (bf16[128,1024]{1,0:T(8,128)(2,1)S(1)}, bf16[128,1024]{1,0:T(8,128)(2,1)}, u32[]{:S(2)}) copy-start(bf16[128,1024]{1,0:T(8,128)(2,1)} %amp_ref.1) | copy-start | bytes 786436
  3.1 60.8 %copy-start.1 = (s32[1,8]{1,0:T(1,128)S(1)}, s32[1,8]{1,0:T(1,128)}, u32[]{:S(2)}) copy-start(s32[1,8]{1,0:T(1,128)} %tiles_ref.2) | copy-start | bytes 100

commit v3 on v2

--- a/solution.py
+++ b/solution.py
@@ -9,6 +9,7 @@
 
 NZ = 6
 NOTE = 16
+LAG = 256.0
 FINE = 8.0
 VMEM = pl.BlockSpec(memory_space=pltpu.VMEM)
 SMEM = pl.BlockSpec(memory_space=pltpu.SMEM)
@@ -27,22 +28,21 @@
 
 
 def pack_kernel(kt, tile, tiles_ref, integrals_ref, out_ref):
-    ones = [tiles_ref[k, 0] for k in range(kt)]
+    ones = [tiles_ref[0, k] for k in range(kt)]
     zeros = [sum(1 - ones[j] for j in range(k + 1)) for k in range(kt)]
-    shifts = []
+    notes = []
     for i in range(NZ):
-        at = i
+        lag = 0
         for o in range(kt - NZ):
-            at = at + (zeros[i + o] > o).astype(jnp.int32)
-        start = pl.multiple_of(at * tile, tile)
+            lag = lag + (zeros[i + o] > o).astype(jnp.int32)
+        start = pl.multiple_of((i + lag) * tile, tile)
         block = integrals_ref[pl.ds(start, tile), :].astype(jnp.float32)
         top = jnp.max(jnp.abs(block), axis=0, keepdims=True)
         shift = jnp.floor(14.99 - jnp.log2(jnp.maximum(top, 1e-37)))
         shift = jnp.clip(shift, 0.0, 120.0)
         out_ref[i * tile : (i + 1) * tile] = to_int16(block * jnp.exp2(shift))
-        shifts.append(shift)
-    mask = [one.astype(jnp.float32) for one in ones]
-    out_ref[NZ * tile :] = note_of(shifts + mask, tile)
+        notes.append(shift + LAG * lag.astype(jnp.float32))
+    out_ref[NZ * tile :] = note_of(notes, tile)
 
 
 def ladder_kernel(kt, tile, tiles_ref, amp_ref, packed_ref, out_ref, masked, full):
@@ -63,20 +63,20 @@
         for j in range(per):
             b = g * per + j
             note = packed_ref[b, NZ * tile :].astype(jnp.int32).astype(jnp.float32)
+            lag = jnp.floor(note / LAG)
+            scale = jnp.exp2(LAG * lag - note)
+            lags = range(kt - NZ + 1)
+            place = [jnp.where(lag == o, scale, 0.0).astype(jnp.bfloat16) for o in lags]
             slots = []
             for i in range(NZ):
-                block = packed_ref[b, i * tile : (i + 1) * tile]
-                block = block.astype(jnp.int32).astype(jnp.float32)
-                slots.append((block * jnp.exp2(-note[i : i + 1])).astype(jnp.bfloat16))
-            zeros = jnp.zeros((1, tile), jnp.float32)
+                block = packed_ref[b, i * tile : (i + 1) * tile].astype(jnp.int32)
+                slots.append(block.astype(jnp.float32).astype(jnp.bfloat16))
             for k in range(kt):
-                one = note[NZ + k : NZ + k + 1]
-                zeros = zeros + (1.0 - one)
                 out = None
-                for o in range(kt - NZ + 1):
-                    if 0 <= k - o < NZ:
-                        here = jnp.where(zeros == o, one, 0.0).astype(jnp.bfloat16)
-                        term = slots[k - o] * here
+                for o in lags:
+                    i = k - o
+                    if 0 <= i < NZ:
+                        term = slots[i] * place[o][i : i + 1]
                         out = term if out is None else out + term
                 full[g, k * tile : (k + 1) * tile, j * tile : (j + 1) * tile] = out
         part = jnp.dot(masked[...], full[g], preferred_element_type=jnp.float32)
@@ -107,10 +107,10 @@
         in_specs=[SMEM, VMEM],
         out_specs=VMEM,
         name="pack",
-    )(int_tiles, integrals)
+    )(int_tiles.reshape(1, kt), integrals)
     everyone = lax.all_gather(packed, "grp")
     per = width // tile
-    step = 2
+    step = 4
     parts = pl.pallas_call(
         functools.partial(ladder_kernel, kt, tile),
         out_shape=jax.ShapeDtypeStruct((owners, rows + NOTE, width), jnp.int16),

time: 98.4 us -> 95.4 us (0.970)
  Pallas kernels: 11.1 us -> 9.44 us
  local copies, waits for them, and re-layouts: 1.33 us -> 0.01 us
    pallas_call x1, Pallas kernels: 7.14 us -> 5.5 us  [on_device(): pl.pallas_call(functools.partial(ladder_kernel, kt, tile), out_shape=jax....]
    unnamed x5 -> x4, local copies, waits for them, and re-layouts: 1.33 us -> 0.01 us
where the time goes in v3:
time: 95.4 us; the launch traced here: 95.2 us
  blocking collectives  85.8 us (90%)
  Pallas kernels  9.44 us (10%)
    all_gather x1, blocking collectives, on_device(): everyone = lax.all_gather(packed, 'grp')  60.8 us
    all_to_all x1, blocking collectives, on_device(): lax.all_to_all(parts, 'mem', 0, 0)  24.9 us
    pallas_call x1, Pallas kernels, on_device(): pl.pallas_call(functools.partial(ladder_kernel, kt, tile), out_shape=jax....  5.5 us
    pallas_call x1, Pallas kernels, on_device(): pl.pallas_call(update_kernel, out_shape=jax.ShapeDtypeStruct((rows, width...  2.21 us

profile of v3, /device:TPU:1, one launch (start us, length us, event | category | flops | bytes accessed | tf_op | source)
XLA Modules:
  0.0 95.2 jit_solution(8641395317695047105)
XLA Ops:
  0.0 1.7 %pack.1 = s16[784,128]{1,0:T(8,128)(2,1)} custom-call(s32[1,8]{1,0:T(1,128)} %bitcast.3, bf16[1024,128]{1,0:T(8,128)(2,1)} %integrals_ref.1), custom_call_target="tpu_custom_call" | custom-call | tf_op jit(solution)/shard_map/pack/pallas_call | solution.py:104
  1.7 0.0 copy-start
  1.7 0.0 copy-start.1
  1.7 60.8 %all-gather.2 = s16[25088,128]{1,0:T(8,128)(2,1)S(1)} all-gather(s16[784,128]{1,0:T(8,128)(2,1)} %pack.1), channel_id=2, replica_groups=mesh['grp'=32,'mem'=16] {'grp'}, dimensions={0}, use_global_device_ids=true | all-gather | bytes 6623232 | tf_op jit(solution)/shard_map/all_gather | solution.py:111
  62.6 0.0 copy-done
  62.6 0.0 copy-done.1
  62.6 5.5 %ladder.1 = s16[16,144,256]{2,1,0:T(8,128)(2,1)S(1)} custom-call(s32[1,8]{1,0:T(1,128)S(1)} %copy-done.1, bf16[128,1024]{1,0:T(8,128)(2,1)S(1)} %copy-done, s16[32,784,128]{2,1,0:T(8,128)(2,1)S(1)} %bitcast.2), custom_call_target="tpu_custom_call" | custom-call | tf_op jit(solution)/shard_map/ladder/pallas_call | solution.py:114
  68.1 24.9 %all_to_all.5.parts_ref = s16[16,144,256]{2,1,0:T(8,128)(2,1)} all-to-all(s16[16,144,256]{2,1,0:T(8,128)(2,1)S(1)} %ladder.1), channel_id=1, replica_groups=mesh['grp'=32,'mem'=16] {'mem'}, dimensions={0} | all-to-all | bytes 2359296 | tf_op jit(solution)/shard_map/all_to_all | solution.py:137
  93.0 2.2 %update.1 = bf16[128,256]{1,0:T(8,128)(2,1)} custom-call(s16[16,144,256]{2,1,0:T(8,128)(2,1)} %all_to_all.5.parts_ref, f32[128,256]{1,0:T(8,128)} %denominators_ref.1), custom_call_target="tpu_custom_call" | custom-call | tf_op jit(solution)/shard_map/update/pallas_call | solution.py:131
Async XLA Ops:
  1.7 60.8 %copy-start = (bf16[128,1024]{1,0:T(8,128)(2,1)S(1)}, bf16[128,1024]{1,0:T(8,128)(2,1)}, u32[]{:S(2)}) copy-start(bf16[128,1024]{1,0:T(8,128)(2,1)} %amp_ref.1) | copy-start | bytes 786436
  1.7 60.8 %copy-start.1 = (s32[1,8]{1,0:T(1,128)S(1)}, s32[1,8]{1,0:T(1,128)}, u32[]{:S(2)}) copy-start(s32[1,8]{1,0:T(1,128)} %tiles_ref.1) | copy-start | bytes 100

commit v4 on v0

v4 whole, which is shorter than its diff:
```python
import functools

import jax
import jax.numpy as jnp
from jax import lax
from jax.experimental import pallas as pl
from jax.experimental.pallas import tpu as pltpu
from jax.sharding import PartitionSpec as P

NZ = 6
NOTE = 16
FINE = 8.0
VMEM = pl.BlockSpec(memory_space=pltpu.VMEM)
SMEM = pl.BlockSpec(memory_space=pltpu.SMEM)


def to_int16(values):
    return jnp.round(values).astype(jnp.int32).astype(jnp.int16)


def note_of(rows, width):
    at = lax.broadcasted_iota(jnp.int32, (NOTE, width), 0)
    note = jnp.zeros((NOTE, width), jnp.float32)
    for i, row in enumerate(rows):
        note = jnp.where(at == i, row, note)
    return note


def pack_kernel(kt, tile, int_ref, amp_tiles_ref, integrals_ref, amp_ref, out_ref, masked_ref):
    ones = [int_ref[0, k] for k in range(kt)]
    zeros = [sum(1 - ones[j] for j in range(k + 1)) for k in range(kt)]
    lags = []
    for i in range(NZ):
        lag = 0
        for o in range(kt - NZ):
            lag = lag + (zeros[i + o] > o).astype(jnp.int32)
        start = pl.multiple_of((i + lag) * tile, tile)
        out_ref[i * tile : (i + 1) * tile] = integrals_ref[pl.ds(start, tile), :]
        lags.append(lag.astype(jnp.float32))
    out_ref[NZ * tile :] = note_of(lags, tile).astype(jnp.bfloat16)
    for k in range(kt):
        cols = slice(k * tile, (k + 1) * tile)
        keep = amp_tiles_ref[0, k].astype(jnp.float32)
        masked_ref[:, cols] = (amp_ref[:, cols].astype(jnp.float32) * keep).astype(
            jnp.bfloat16
        )


def ladder_kernel(kt, tile, amp_ref, left_ref, right_ref, *rest):
    out_ref, full = rest[-2:]
    pieces, height, width = out_ref.shape
    rows = height - NOTE
    lags = range(kt - NZ + 1)
    for j, block_ref in enumerate((left_ref, right_ref)):
        note = block_ref[NZ * tile :].astype(jnp.float32)
        place = [jnp.where(note == o, 1.0, 0.0).astype(jnp.bfloat16) for o in lags]
        slots = [block_ref[i * tile : (i + 1) * tile] for i in range(NZ)]
        for k in range(kt):
            out = None
            for o in lags:
                i = k - o
                if 0 <= i < NZ:
                    term = slots[i] * place[o][i : i + 1]
                    out = term if out is None else out + term
            full[k * tile : (k + 1) * tile, j * tile : (j + 1) * tile] = out
    sums = jnp.dot(amp_ref[...], full[...], preferred_element_type=jnp.float32)
    for p in range(pieces):
        part = sums[p * rows : (p + 1) * rows]
        top = jnp.max(jnp.abs(part), axis=0, keepdims=True)
        shift = jnp.floor(FINE * (14.999 - jnp.log2(jnp.maximum(top, 1e-30))))
        out_ref[p, :rows] = to_int16(part * jnp.exp2(shift / FINE))
        out_ref[p, rows:] = to_int16(note_of([shift], width))


def sum_kernel(core_ref, parts_ref, first_ref, second_ref):
    rows, half = first_ref.shape
    total = jnp.zeros((rows, 2 * half), jnp.float32)
    for i in range(parts_ref.shape[0]):
        note = parts_ref[i, rows:].astype(jnp.int32).astype(jnp.float32)
        part = parts_ref[i, :rows].astype(jnp.int32).astype(jnp.float32)
        total = total + part * jnp.exp2(note[:1] / -FINE)
    left, right = total[:, :half], total[:, half:]
    swap = core_ref[0, 0] == 1
    first_ref[...] = jnp.where(swap, right, left)
    second_ref[...] = jnp.where(swap, left, right)


def update_kernel(swap_ref, first_ref, second_ref, denominators_ref, out_ref):
    half = first_ref.shape[1]
    swap = swap_ref[0, 0] == 1
    first, second = first_ref[...], second_ref[...]
    left = jnp.where(swap, second, first) / denominators_ref[:, :half]
    right = jnp.where(swap, first, second) / denominators_ref[:, half:]
    out_ref[:, :half] = left.astype(out_ref.dtype)
    out_ref[:, half:] = right.astype(out_ref.dtype)


def routes(planes, owners):
    first, second = [], []
    for z in range(planes):
        for c in range(2):
            for m in range(owners):
                step, row = divmod(m, 4)
                if step < 3:
                    to = [(z + (2 * c - 1) * 2 * (step + 1)) % planes] * 2
                else:
                    to = [z, (z + planes // 2) % planes][:: 1 - 2 * c]
                grp = 2 * (z ^ (row // 2)) + (c ^ (row % 2))
                me = (2 * z + c) * owners + m
                first.append((me, grp * owners + to[0]))
                second.append((me, grp * owners + to[1]))
    return first, second


def on_device(amplitudes, amp_tiles, integrals, int_tiles, denominators):
    rows, depth = amplitudes.shape
    kt = int_tiles.shape[0]
    tile = depth // kt
    groups, owners = lax.axis_size("grp"), lax.axis_size("mem")
    planes, width = groups // 2, denominators.shape[1]
    grp, mem = lax.axis_index("grp"), lax.axis_index("mem")
    plane, core = grp // 2, grp % 2

    other_core = [(g, g ^ 1) for g in range(groups)]
    other_plane = [(g, g ^ 2) for g in range(groups)]
    onward = [(g, (g + (4 if g % 2 == 0 else -4)) % groups) for g in range(groups)]

    own, masked = pl.pallas_call(
        functools.partial(pack_kernel, kt, tile),
        out_shape=(
            jax.ShapeDtypeStruct((NZ * tile + NOTE, tile), jnp.bfloat16),
            jax.ShapeDtypeStruct((rows, depth), jnp.bfloat16),
        ),
        in_specs=[SMEM, SMEM, VMEM, VMEM],
        out_specs=(VMEM, VMEM),
        name="pack",
    )(int_tiles.reshape(1, kt), amp_tiles, integrals, amplitudes)
    partner = lax.ppermute(own, "grp", other_core)
    lefts, rights = [own], [partner]
    for s in range(4):
        lefts.append(lax.ppermute(lefts[-1], "grp", onward))
        if s < 3:
            rights.append(lax.ppermute(rights[-1], "grp", onward))

    beside = lax.ppermute(masked, "grp", other_core)
    across = lax.ppermute(masked, "grp", other_plane)
    amps = jnp.concatenate(
        [masked, beside, across, lax.ppermute(across, "grp", other_core)], axis=0
    )

    parts = None
    for s in range(4):
        pair = (lefts[s + 1], rights[s + 1]) if s < 3 else (own, lefts[4])
        parts = pl.pallas_call(
            functools.partial(ladder_kernel, kt, tile),
            out_shape=jax.ShapeDtypeStruct((owners, rows + NOTE, width), jnp.int16),
            grid=(1,),
            in_specs=[
                pl.BlockSpec((4 * rows, depth), lambda i: (0, 0)),
                pl.BlockSpec((NZ * tile + NOTE, tile), lambda i: (0, 0)),
                pl.BlockSpec((NZ * tile + NOTE, tile), lambda i: (0, 0)),
            ]
            + ([] if parts is None else [pl.BlockSpec(memory_space=pl.ANY)]),
            out_specs=pl.BlockSpec(
                (4, rows + NOTE, width), functools.partial(lambda s, i: (s, 0, 0), s)
            ),
            scratch_shapes=[pltpu.VMEM((depth, width), jnp.bfloat16)],
            input_output_aliases={} if parts is None else {3: 0},
            cost_estimate=pl.CostEstimate(
                flops=8 * rows * depth * width, bytes_accessed=2**21, transcendentals=0
            ),
            compiler_params=pltpu.CompilerParams(vmem_limit_bytes=32 * 2**20),
            name="ladder",
        )(amps, *pair, *([] if parts is None else [parts]))

    half = jax.ShapeDtypeStruct((rows, tile), jnp.float32)
    first, second = pl.pallas_call(
        sum_kernel,
        out_shape=(half, half),
        in_specs=[SMEM, VMEM],
        out_specs=(VMEM, VMEM),
        name="sum",
    )(core.reshape(1, 1), lax.all_to_all(parts, "mem", 0, 0))
    to_first, to_second = routes(planes, owners)
    first = lax.ppermute(first, ("grp", "mem"), to_first)
    second = lax.ppermute(second, ("grp", "mem"), to_second)
    source = jnp.bitwise_xor(plane, jnp.bitwise_and(plane + mem, 1))
    swap = (mem == (source + planes // 2) % planes).astype(jnp.int32)
    return pl.pallas_call(
        update_kernel,
        out_shape=jax.ShapeDtypeStruct((rows, width), jnp.bfloat16),
        in_specs=[SMEM, VMEM, VMEM, VMEM],
        out_specs=VMEM,
        name="update",
    )(swap.reshape(1, 1), first, second, denominators)


def solution(mesh):
    return jax.shard_map(
        on_device,
        mesh=mesh,
        in_specs=(
            P("grp", "mem"),
            P("grp", "mem"),
            P("mem", "grp"),
            P("mem", "grp"),
            P("grp", "mem"),
        ),
        out_specs=P("grp", "mem"),
        check_vma=False,
    )
```

time: 211 us -> 105 us (0.50)
  the two profiles are of different devices: /device:TPU:1 before, /device:TPU:2 now
where the time goes in v4:
time: 105 us; the launch traced here: 104 us
  starting transfers between devices  46.9 us (45%)
  waiting for transfers between devices  43.6 us (42%)
  Pallas kernels  11 us (10%)
  local copies, waits for them, and re-layouts  2.7 us (3%)
    all_to_all x1, waiting for transfers between devices, on_device(): lax.all_to_all(parts, 'mem', 0, 0)  16.3 us
    ppermute x3, waiting for transfers between devices, on_device(): rights.append(lax.ppermute(rights[-1], 'grp', onward))  14.7 us
    ppermute x4, starting transfers between devices, on_device(): lefts.append(lax.ppermute(lefts[-1], 'grp', onward))  13.3 us
    ppermute x3, starting transfers between devices, on_device(): rights.append(lax.ppermute(rights[-1], 'grp', onward))  10.2 us
    all_to_all x1, starting transfers between devices, on_device(): lax.all_to_all(parts, 'mem', 0, 0)  7.48 us
    ppermute x1, waiting for transfers between devices, on_device(): first = lax.ppermute(first, ('grp', 'mem'), to_first)  5.49 us
    pallas_call x4, Pallas kernels, on_device(): pl.pallas_call(functools.partial(ladder_kernel, kt, tile), out_shape=jax....  5.31 us
    ppermute x1, starting transfers between devices, on_device(): beside = lax.ppermute(masked, 'grp', other_core)  4.38 us
  transfers between devices with their start and end apart: 14, of which 10 were waited for; matrix products, arithmetic and copies ran while one was open for 1% of the time, Pallas kernels for 4%

profile of v4, /device:TPU:2, one launch (start us, length us, event | category | flops | bytes accessed | tf_op | source)
XLA Modules:
  0.0 104.4 jit_solution(4719023711701603516)
XLA Ops:
  0.0 1.8 %pack.1 = (bf16[784,128]{1,0:T(8,128)(2,1)}, bf16[128,1024]{1,0:T(8,128)(2,1)}) custom-call(s32[1,8]{1,0:T(1,128)} %bitcast.3, s32[1,8]{1,0:T(1,128)} %amp_tiles_ref.1, bf16[1024,128]{1,0:T(8,128)(2,1)} %integrals_ref.1, bf16[128,1024]{1,0:T(8,128)(2,1)} %amp_ref.1), custom_call_target="tpu_custom_call" | custom-call | tf_op jit(solution)/shard_map/pack/pallas_call | solution.py:128
  1.8 1.9 %collective-permute-start.7 = (bf16[784,128]{1,0:T(8,128)(2,1)}, bf16[784,128]{1,0:T(8,128)(2,1)S(1)}, u32[]{:S(2)}, u32[]{:S(2)}) collective-permute-start(bf16[784,128]{1,0:T(8,128)(2,1)} %get-tuple-element.10.left_ref), channel_id=1, source_target_pairs={{0,16},{16,0},{32,48},{48,32},{64,80},{80,64},{96,112},{112,96},{1... | collective-permute-start | bytes 602120 | tf_op jit(solution)/shard_map/ppermute | solution.py:138
  3.8 5.2 %collective-permute-start.3 = (bf16[784,128]{1,0:T(8,128)(2,1)}, bf16[784,128]{1,0:T(8,128)(2,1)S(1)}, u32[]{:S(2)}, u32[]{:S(2)}) collective-permute-start(bf16[784,128]{1,0:T(8,128)(2,1)} %get-tuple-element.10.left_ref), channel_id=1, source_target_pairs={{0,64},{16,464},{32,96},{48,496},{64,128},{80,16},{96,160},{112,48... | collective-permute-start | bytes 602120 | tf_op jit(solution)/shard_map/ppermute | solution.py:141
  9.0 3.8 %collective-permute-start.1 = (bf16[128,1024]{1,0:T(8,128)(2,1)}, bf16[128,1024]{1,0:T(8,128)(2,1)S(1)}, u32[]{:S(2)}, u32[]{:S(2)}) collective-permute-start(bf16[128,1024]{1,0:T(8,128)(2,1)} %get-tuple-element.9), channel_id=1, source_target_pairs={{0,32},{16,48},{32,0},{48,16},{64,96},{80,112},{96,64},{112,80},{1... | collective-permute-start | bytes 786440 | tf_op jit(solution)/shard_map/ppermute | solution.py:146
  12.8 0.0 collective-permute-done.7
  12.8 6.4 %collective-permute-start.8 = (bf16[784,128]{1,0:T(8,128)(2,1)S(1)}, bf16[784,128]{1,0:T(8,128)(2,1)S(1)}, u32[]{:S(2)}, u32[]{:S(2)}) collective-permute-start(bf16[784,128]{1,0:T(8,128)(2,1)S(1)} %collective-permute-done.7), channel_id=1, source_target_pairs={{0,64},{16,464},{32,96},{48,496},{64,128},{80,16},{96,160},{112,48... | collective-permute-start | bytes 602120 | tf_op jit(solution)/shard_map/ppermute | solution.py:143
  19.2 0.9 collective-permute-done.3.left_ref
  20.1 4.3 %collective-permute-start.4 = (bf16[784,128]{1,0:T(8,128)(2,1)S(1)}, bf16[784,128]{1,0:T(8,128)(2,1)S(1)}, u32[]{:S(2)}, u32[]{:S(2)}) collective-permute-start(bf16[784,128]{1,0:T(8,128)(2,1)S(1)} %collective-permute-done.3.left_ref), channel_id=1, source_target_pairs={{0,64},{16,464},{32,96},{48,496},{64,128},{80,16},{96,160},{112,48... | collective-permute-start | bytes 602120 | tf_op jit(solution)/shard_map/ppermute | solution.py:141
  24.4 4.4 %collective-permute-start = (bf16[128,1024]{1,0:T(8,128)(2,1)}, bf16[128,1024]{1,0:T(8,128)(2,1)S(1)}, u32[]{:S(2)}, u32[]{:S(2)}) collective-permute-start(bf16[128,1024]{1,0:T(8,128)(2,1)} %get-tuple-element.9), channel_id=1, source_target_pairs={{0,16},{16,0},{32,48},{48,32},{64,80},{80,64},{96,112},{112,96},{1... | collective-permute-start | bytes 786440 | tf_op jit(solution)/shard_map/ppermute | solution.py:145
  28.8 0.0 collective-permute-done.1
  28.8 1.9 %collective-permute-start.2 = (bf16[128,1024]{1,0:T(8,128)(2,1)S(1)}, bf16[128,1024]{1,0:T(8,128)(2,1)S(1)}, u32[]{:S(2)}, u32[]{:S(2)}) collective-permute-start(bf16[128,1024]{1,0:T(8,128)(2,1)S(1)} %collective-permute-done.1), channel_id=1, source_target_pairs={{0,16},{16,0},{32,48},{48,32},{64,80},{80,64},{96,112},{112,96},{1... | collective-permute-start | bytes 786440 | tf_op jit(solution)/shard_map/ppermute | solution.py:148
  30.7 3.3 %collective-permute-done.8.right_ref = bf16[784,128]{1,0:T(8,128)(2,1)S(1)} collective-permute-done((bf16[784,128]{1,0:T(8,128)(2,1)S(1)}, bf16[784,128]{1,0:T(8,128)(2,1)S(1)}, u32[]{:S(2)}, u32[]{:S(2)}) %collective-permute-start.8) | collective-permute-done | bytes 200736 | tf_op jit(solution)/shard_map/ppermute | solution.py:143
  34.0 1.9 %collective-permute-start.9 = (bf16[784,128]{1,0:T(8,128)(2,1)S(1)}, bf16[784,128]{1,0:T(8,128)(2,1)S(1)}, u32[]{:S(2)}, u32[]{:S(2)}) collective-permute-start(bf16[784,128]{1,0:T(8,128)(2,1)S(1)} %collective-permute-done.8.right_ref), channel_id=1, source_target_pairs={{0,64},{16,464},{32,96},{48,496},{64,128},{80,16},{96,160},{112,48... | collective-permute-start | bytes 602120 | tf_op jit(solution)/shard_map/ppermute | solution.py:143
  35.9 0.2 collective-permute-done.4.left_ref
  36.1 1.9 %collective-permute-start.5 = (bf16[784,128]{1,0:T(8,128)(2,1)S(1)}, bf16[784,128]{1,0:T(8,128)(2,1)S(1)}, u32[]{:S(2)}, u32[]{:S(2)}) collective-permute-start(bf16[784,128]{1,0:T(8,128)(2,1)S(1)} %collective-permute-done.4.left_ref), channel_id=1, source_target_pairs={{0,64},{16,464},{32,96},{48,496},{64,128},{80,16},{96,160},{112,48... | collective-permute-start | bytes 602120 | tf_op jit(solution)/shard_map/ppermute | solution.py:141
  38.0 1.0 constant_dynamic-update-slice_fusion.3
  39.0 0.0 collective-permute-done
  39.0 8.0 %collective-permute-done.9.right_ref = bf16[784,128]{1,0:T(8,128)(2,1)S(1)} collective-permute-done((bf16[784,128]{1,0:T(8,128)(2,1)S(1)}, bf16[784,128]{1,0:T(8,128)(2,1)S(1)}, u32[]{:S(2)}, u32[]{:S(2)}) %collective-permute-start.9) | collective-permute-done | bytes 200736 | tf_op jit(solution)/shard_map/ppermute | solution.py:143
  47.1 1.9 %collective-permute-start.10 = (bf16[784,128]{1,0:T(8,128)(2,1)S(1)}, bf16[784,128]{1,0:T(8,128)(2,1)S(1)}, u32[]{:S(2)}, u32[]{:S(2)}) collective-permute-start(bf16[784,128]{1,0:T(8,128)(2,1)S(1)} %collective-permute-done.9.right_ref), channel_id=1, source_target_pairs={{0,64},{16,464},{32,96},{48,496},{64,128},{80,16},{96,160},{112,48... | collective-permute-start | bytes 602120 | tf_op jit(solution)/shard_map/ppermute | solution.py:143
  49.0 0.3 collective-permute-done.5.left_ref
  49.3 2.0 %collective-permute-start.6 = (bf16[784,128]{1,0:T(8,128)(2,1)S(1)}, bf16[784,128]{1,0:T(8,128)(2,1)S(1)}, u32[]{:S(2)}, u32[]{:S(2)}) collective-permute-start(bf16[784,128]{1,0:T(8,128)(2,1)S(1)} %collective-permute-done.5.left_ref), channel_id=1, source_target_pairs={{0,64},{16,464},{32,96},{48,496},{64,128},{80,16},{96,160},{112,48... | collective-permute-start | bytes 602120 | tf_op jit(solution)/shard_map/ppermute | solution.py:141
  51.3 0.0 collective-permute-done.2
  51.3 1.3 %ladder.4.rest_0_ = s16[16,144,256]{2,1,0:T(8,128)(2,1)} custom-call(bf16[512,1024]{1,0:T(8,128)(2,1)S(1)} %constant_dynamic-update-slice_fusion.amp_ref, bf16[784,128]{1,0:T(8,128)(2,1)S(1)} %collective-permute-done.3.left_ref, bf16[784,128]{1,0:T(8,128)(2,1)S(1)} %collective-permute-done.8.right_ref), custom_call_target="tpu_custom_call" | custom-call | flops 268435456 | bytes 2097152 | tf_op jit(solution)/shard_map/ladder/pallas_call | solution.py:154
  52.7 1.3 %ladder.5.rest_0_ = s16[16,144,256]{2,1,0:T(8,128)(2,1)} custom-call(bf16[512,1024]{1,0:T(8,128)(2,1)S(1)} %constant_dynamic-update-slice_fusion.amp_ref, bf16[784,128]{1,0:T(8,128)(2,1)S(1)} %collective-permute-done.4.left_ref, bf16[784,128]{1,0:T(8,128)(2,1)S(1)} %collective-permute-done.9.right_ref, ...), custom_call_target="tpu_custom_call", output_to_operand_aliasing={{}: (3, {})} | custom-call | flops 268435456 | bytes 2097152 | tf_op jit(solution)/shard_map/ladder/pallas_call | solution.py:154
  54.0 0.0 copy-start
  54.0 3.5 %collective-permute-done.10.right_ref = bf16[784,128]{1,0:T(8,128)(2,1)S(1)} collective-permute-done((bf16[784,128]{1,0:T(8,128)(2,1)S(1)}, bf16[784,128]{1,0:T(8,128)(2,1)S(1)}, u32[]{:S(2)}, u32[]{:S(2)}) %collective-permute-start.10) | collective-permute-done | bytes 200736 | tf_op jit(solution)/shard_map/ppermute | solution.py:143
  57.5 1.3 %ladder.6.rest_0_ = s16[16,144,256]{2,1,0:T(8,128)(2,1)} custom-call(bf16[512,1024]{1,0:T(8,128)(2,1)S(1)} %constant_dynamic-update-slice_fusion.amp_ref, bf16[784,128]{1,0:T(8,128)(2,1)S(1)} %collective-permute-done.5.left_ref, bf16[784,128]{1,0:T(8,128)(2,1)S(1)} %collective-permute-done.10.right_ref, ...), custom_call_target="tpu_custom_call", output_to_operand_aliasing={{}: (3, {})} | custom-call | flops 268435456 | bytes 2097152 | tf_op jit(solution)/shard_map/ladder/pallas_call | solution.py:154
  58.8 2.2 %collective-permute-done.6.right_ref = bf16[784,128]{1,0:T(8,128)(2,1)S(1)} collective-permute-done((bf16[784,128]{1,0:T(8,128)(2,1)S(1)}, bf16[784,128]{1,0:T(8,128)(2,1)S(1)}, u32[]{:S(2)}, u32[]{:S(2)}) %collective-permute-start.6) | collective-permute-done | bytes 200736 | tf_op jit(solution)/shard_map/ppermute | solution.py:141
  61.0 0.0 copy-done
  61.0 1.3 %ladder.7 = s16[16,144,256]{2,1,0:T(8,128)(2,1)} custom-call(bf16[512,1024]{1,0:T(8,128)(2,1)S(1)} %constant_dynamic-update-slice_fusion.amp_ref, bf16[784,128]{1,0:T(8,128)(2,1)S(1)} %copy-done, bf16[784,128]{1,0:T(8,128)(2,1)S(1)} %collective-permute-done.6.right_ref, s16[16,144,256]{2,1,0:T(8,128)(2,1)} %ladder.6.rest_0_), custom_call_target="tpu_custom_call", output_to_operand_aliasing={{}: (3, {})} | custom-call | flops 268435456 | bytes 2097152 | tf_op jit(solution)/shard_map/ladder/pallas_call | solution.py:154
  62.3 7.5 %all-to-all-start = ((s16[16,144,256]{2,1,0:T(8,128)(2,1)}), s16[16,144,256]{2,1,0:T(8,128)(2,1)S(1)}, u32[]{:S(2)}, u32[]{:S(2)}) async-start(s16[16,144,256]{2,1,0:T(8,128)(2,1)} %ladder.7), calls=%async_computation | async-start | bytes 2359296 | tf_op jit(solution)/shard_map/all_to_all | solution.py:183
  69.8 16.3 %all-to-all-done.parts_ref = s16[16,144,256]{2,1,0:T(8,128)(2,1)S(1)} async-done(((s16[16,144,256]{2,1,0:T(8,128)(2,1)}), s16[16,144,256]{2,1,0:T(8,128)(2,1)S(1)}, u32[]{:S(2)}, u32[]{:S(2)}) %all-to-all-start) | async-done | bytes 1179680 | tf_op jit(solution)/shard_map/all_to_all | solution.py:183
  86.1 0.0 copy-start.1
  86.1 1.0 %copy-done.1 = s16[16,144,256]{2,1,0:T(8,128)(2,1)} copy-done((s16[16,144,256]{2,1,0:T(8,128)(2,1)}, s16[16,144,256]{2,1,0:T(8,128)(2,1)S(1)}, u32[]{:S(2)}) %copy-start.1) | copy-done | bytes 1179672
  87.2 2.2 %sum.1 = (f32[128,128]{1,0:T(8,128)}, f32[128,128]{1,0:T(8,128)}) custom-call(s32[1,1]{1,0:T(1,128)} %bitcast.1.core_ref, s16[16,144,256]{2,1,0:T(8,128)(2,1)} %copy-done.1), custom_call_target="tpu_custom_call" | custom-call | tf_op jit(solution)/shard_map/sum/pallas_call | solution.py:177
  89.4 1.9 %collective-permute-start.11 = (f32[128,128]{1,0:T(8,128)}, f32[128,128]{1,0:T(8,128)S(1)}, u32[]{:S(2)}, u32[]{:S(2)}) collective-permute-start(f32[128,128]{1,0:T(8,128)} %get-tuple-element.11), channel_id=1, source_target_pairs={{0,14},{1,30},{2,46},{3,62},{4,12},{5,28},{6,44},{7,60},{8,10},{9,... | collective-permute-start | bytes 196616 | tf_op jit(solution)/shard_map/ppermute | solution.py:185
  91.3 1.9 %collective-permute-start.12 = (f32[128,128]{1,0:T(8,128)}, f32[128,128]{1,0:T(8,128)S(1)}, u32[]{:S(2)}, u32[]{:S(2)}) collective-permute-start(f32[128,128]{1,0:T(8,128)} %get-tuple-element.12), channel_id=1, source_target_pairs={{0,14},{1,30},{2,46},{3,62},{4,12},{5,28},{6,44},{7,60},{8,10},{9,... | collective-permute-start | bytes 196616 | tf_op jit(solution)/shard_map/ppermute | solution.py:186
  93.3 5.5 %collective-permute-done.11.first_ref = f32[128,128]{1,0:T(8,128)S(1)} collective-permute-done((f32[128,128]{1,0:T(8,128)}, f32[128,128]{1,0:T(8,128)S(1)}, u32[]{:S(2)}, u32[]{:S(2)}) %collective-permute-start.11) | collective-permute-done | bytes 65568 | tf_op jit(solution)/shard_map/ppermute | solution.py:185
  98.8 0.0 copy-start.2
  98.8 3.4 %collective-permute-done.12.second_ref = f32[128,128]{1,0:T(8,128)S(1)} collective-permute-done((f32[128,128]{1,0:T(8,128)}, f32[128,128]{1,0:T(8,128)S(1)}, u32[]{:S(2)}, u32[]{:S(2)}) %collective-permute-start.12) | collective-permute-done | bytes 65568 | tf_op jit(solution)/shard_map/ppermute | solution.py:186
  102.2 0.0 copy-start.3
  102.2 0.0 copy-done.2
  102.2 0.6 copy-done.3
  102.8 1.6 %update.1 = bf16[128,256]{1,0:T(8,128)(2,1)} custom-call(s32[1,1]{1,0:T(1,128)} %bitcast.swap_ref, f32[128,128]{1,0:T(8,128)} %copy-done.2, f32[128,128]{1,0:T(8,128)} %copy-done.3, f32[128,256]{1,0:T(8,128)} %denominators_ref.1), custom_call_target="tpu_custom_call" | custom-call | tf_op jit(solution)/shard_map/update/pallas_call | solution.py:189
  (3 shorter events, 0.1 us)
Async XLA Ops:
  1.8 10.9 %collective-permute-start.7 = (bf16[784,128]{1,0:T(8,128)(2,1)}, bf16[784,128]{1,0:T(8,128)(2,1)S(1)}, u32[]{:S(2)}, u32[]{:S(2)}) collective-permute-start(bf16[784,128]{1,0:T(8,128)(2,1)} %get-tuple-element.10.left_ref), channel_id=1, source_target_pairs={{0,16},{16,0},{32,48},{48,32},{64,80},{80,64},{96,112},{112,96},{1... | collective-permute-start | bytes 602120 | tf_op jit(solution)/shard_map/ppermute | solution.py:138
  3.8 16.3 %collective-permute-start.3 = (bf16[784,128]{1,0:T(8,128)(2,1)}, bf16[784,128]{1,0:T(8,128)(2,1)S(1)}, u32[]{:S(2)}, u32[]{:S(2)}) collective-permute-start(bf16[784,128]{1,0:T(8,128)(2,1)} %get-tuple-element.10.left_ref), channel_id=1, source_target_pairs={{0,64},{16,464},{32,96},{48,496},{64,128},{80,16},{96,160},{112,48... | collective-permute-start | bytes 602120 | tf_op jit(solution)/shard_map/ppermute | solution.py:141
  9.0 19.8 %collective-permute-start.1 = (bf16[128,1024]{1,0:T(8,128)(2,1)}, bf16[128,1024]{1,0:T(8,128)(2,1)S(1)}, u32[]{:S(2)}, u32[]{:S(2)}) collective-permute-start(bf16[128,1024]{1,0:T(8,128)(2,1)} %get-tuple-element.9), channel_id=1, source_target_pairs={{0,32},{16,48},{32,0},{48,16},{64,96},{80,112},{96,64},{112,80},{1... | collective-permute-start | bytes 786440 | tf_op jit(solution)/shard_map/ppermute | solution.py:146
  12.8 21.2 %collective-permute-start.8 = (bf16[784,128]{1,0:T(8,128)(2,1)S(1)}, bf16[784,128]{1,0:T(8,128)(2,1)S(1)}, u32[]{:S(2)}, u32[]{:S(2)}) collective-permute-start(bf16[784,128]{1,0:T(8,128)(2,1)S(1)} %collective-permute-done.7), channel_id=1, source_target_pairs={{0,64},{16,464},{32,96},{48,496},{64,128},{80,16},{96,160},{112,48... | collective-permute-start | bytes 602120 | tf_op jit(solution)/shard_map/ppermute | solution.py:143
  20.1 16.0 %collective-permute-start.4 = (bf16[784,128]{1,0:T(8,128)(2,1)S(1)}, bf16[784,128]{1,0:T(8,128)(2,1)S(1)}, u32[]{:S(2)}, u32[]{:S(2)}) collective-permute-start(bf16[784,128]{1,0:T(8,128)(2,1)S(1)} %collective-permute-done.3.left_ref), channel_id=1, source_target_pairs={{0,64},{16,464},{32,96},{48,496},{64,128},{80,16},{96,160},{112,48... | collective-permute-start | bytes 602120 | tf_op jit(solution)/shard_map/ppermute | solution.py:141
  24.4 14.6 %collective-permute-start = (bf16[128,1024]{1,0:T(8,128)(2,1)}, bf16[128,1024]{1,0:T(8,128)(2,1)S(1)}, u32[]{:S(2)}, u32[]{:S(2)}) collective-permute-start(bf16[128,1024]{1,0:T(8,128)(2,1)} %get-tuple-element.9), channel_id=1, source_target_pairs={{0,16},{16,0},{32,48},{48,32},{64,80},{80,64},{96,112},{112,96},{1... | collective-permute-start | bytes 786440 | tf_op jit(solution)/shard_map/ppermute | solution.py:145
  28.8 22.5 %collective-permute-start.2 = (bf16[128,1024]{1,0:T(8,128)(2,1)S(1)}, bf16[128,1024]{1,0:T(8,128)(2,1)S(1)}, u32[]{:S(2)}, u32[]{:S(2)}) collective-permute-start(bf16[128,1024]{1,0:T(8,128)(2,1)S(1)} %collective-permute-done.1), channel_id=1, source_target_pairs={{0,16},{16,0},{32,48},{48,32},{64,80},{80,64},{96,112},{112,96},{1... | collective-permute-start | bytes 786440 | tf_op jit(solution)/shard_map/ppermute | solution.py:148
  34.0 13.1 %collective-permute-start.9 = (bf16[784,128]{1,0:T(8,128)(2,1)S(1)}, bf16[784,128]{1,0:T(8,128)(2,1)S(1)}, u32[]{:S(2)}, u32[]{:S(2)}) collective-permute-start(bf16[784,128]{1,0:T(8,128)(2,1)S(1)} %collective-permute-done.8.right_ref), channel_id=1, source_target_pairs={{0,64},{16,464},{32,96},{48,496},{64,128},{80,16},{96,160},{112,48... | collective-permute-start | bytes 602120 | tf_op jit(solution)/shard_map/ppermute | solution.py:143
  36.1 13.2 %collective-permute-start.5 = (bf16[784,128]{1,0:T(8,128)(2,1)S(1)}, bf16[784,128]{1,0:T(8,128)(2,1)S(1)}, u32[]{:S(2)}, u32[]{:S(2)}) collective-permute-start(bf16[784,128]{1,0:T(8,128)(2,1)S(1)} %collective-permute-done.4.left_ref), channel_id=1, source_target_pairs={{0,64},{16,464},{32,96},{48,496},{64,128},{80,16},{96,160},{112,48... | collective-permute-start | bytes 602120 | tf_op jit(solution)/shard_map/ppermute | solution.py:141
  47.1 10.4 %collective-permute-start.10 = (bf16[784,128]{1,0:T(8,128)(2,1)S(1)}, bf16[784,128]{1,0:T(8,128)(2,1)S(1)}, u32[]{:S(2)}, u32[]{:S(2)}) collective-permute-start(bf16[784,128]{1,0:T(8,128)(2,1)S(1)} %collective-permute-done.9.right_ref), channel_id=1, source_target_pairs={{0,64},{16,464},{32,96},{48,496},{64,128},{80,16},{96,160},{112,48... | collective-permute-start | bytes 602120 | tf_op jit(solution)/shard_map/ppermute | solution.py:143
  49.3 11.7 %collective-permute-start.6 = (bf16[784,128]{1,0:T(8,128)(2,1)S(1)}, bf16[784,128]{1,0:T(8,128)(2,1)S(1)}, u32[]{:S(2)}, u32[]{:S(2)}) collective-permute-start(bf16[784,128]{1,0:T(8,128)(2,1)S(1)} %collective-permute-done.5.left_ref), channel_id=1, source_target_pairs={{0,64},{16,464},{32,96},{48,496},{64,128},{80,16},{96,160},{112,48... | collective-permute-start | bytes 602120 | tf_op jit(solution)/shard_map/ppermute | solution.py:141
  54.0 7.0 %copy-start = (bf16[784,128]{1,0:T(8,128)(2,1)S(1)}, bf16[784,128]{1,0:T(8,128)(2,1)}, u32[]{:S(2)}) copy-start(bf16[784,128]{1,0:T(8,128)(2,1)} %get-tuple-element.10.left_ref) | copy-start | bytes 602116
  62.3 23.8 %all-to-all-start = ((s16[16,144,256]{2,1,0:T(8,128)(2,1)}), s16[16,144,256]{2,1,0:T(8,128)(2,1)S(1)}, u32[]{:S(2)}, u32[]{:S(2)}) async-start(s16[16,144,256]{2,1,0:T(8,128)(2,1)} %ladder.7), calls=%async_computation | async-start | bytes 2359296 | tf_op jit(solution)/shard_map/all_to_all | solution.py:183
  86.1 1.0 %copy-start.1 = (s16[16,144,256]{2,1,0:T(8,128)(2,1)}, s16[16,144,256]{2,1,0:T(8,128)(2,1)S(1)}, u32[]{:S(2)}) copy-start(s16[16,144,256]{2,1,0:T(8,128)(2,1)S(1)} %all-to-all-done.parts_ref) | copy-start | bytes 3538948
  89.4 9.4 %collective-permute-start.11 = (f32[128,128]{1,0:T(8,128)}, f32[128,128]{1,0:T(8,128)S(1)}, u32[]{:S(2)}, u32[]{:S(2)}) collective-permute-start(f32[128,128]{1,0:T(8,128)} %get-tuple-element.11), channel_id=1, source_target_pairs={{0,14},{1,30},{2,46},{3,62},{4,12},{5,28},{6,44},{7,60},{8,10},{9,... | collective-permute-start | bytes 196616 | tf_op jit(solution)/shard_map/ppermute | solution.py:185
  91.3 10.8 %collective-permute-start.12 = (f32[128,128]{1,0:T(8,128)}, f32[128,128]{1,0:T(8,128)S(1)}, u32[]{:S(2)}, u32[]{:S(2)}) collective-permute-start(f32[128,128]{1,0:T(8,128)} %get-tuple-element.12), channel_id=1, source_target_pairs={{0,14},{1,30},{2,46},{3,62},{4,12},{5,28},{6,44},{7,60},{8,10},{9,... | collective-permute-start | bytes 196616 | tf_op jit(solution)/shard_map/ppermute | solution.py:186
  98.8 3.4 %copy-start.2 = (f32[128,128]{1,0:T(8,128)}, f32[128,128]{1,0:T(8,128)S(1)}, u32[]{:S(2)}) copy-start(f32[128,128]{1,0:T(8,128)S(1)} %collective-permute-done.11.first_ref) | copy-start | bytes 196612
  102.2 0.6 copy-start.3

commit v5 on v3

--- a/solution.py
+++ b/solution.py
@@ -78,22 +78,12 @@
                     if 0 <= i < NZ:
                         term = slots[i] * place[o][i : i + 1]
                         out = term if out is None else out + term
-                full[g, k * tile : (k + 1) * tile, j * tile : (j + 1) * tile] = out
-        part = jnp.dot(masked[...], full[g], preferred_element_type=jnp.float32)
+                full[g % full.shape[0], k * tile : (k + 1) * tile, j * tile : (j + 1) * tile] = out
+        part = jnp.dot(masked[...], full[g % full.shape[0]], preferred_element_type=jnp.float32)
         top = jnp.max(jnp.abs(part), axis=0, keepdims=True)
         shift = jnp.floor(FINE * (14.999 - jnp.log2(jnp.maximum(top, 1e-30))))
         out_ref[g, :rows] = to_int16(part * jnp.exp2(shift / FINE))
         out_ref[g, rows:] = note_of([shift], part.shape[1])
-
-
-def update_kernel(parts_ref, denominators_ref, out_ref):
-    rows = denominators_ref.shape[0]
-    total = jnp.zeros(denominators_ref.shape, jnp.float32)
-    for i in range(parts_ref.shape[0]):
-        note = parts_ref[i, rows:].astype(jnp.int32).astype(jnp.float32)
-        part = parts_ref[i, :rows].astype(jnp.int32).astype(jnp.float32)
-        total = total + part * jnp.exp2(note[:1] / -FINE)
-    out_ref[...] = (total / denominators_ref[...]).astype(out_ref.dtype)
 
 
 def on_device(amplitudes, amp_tiles, integrals, int_tiles, denominators):
@@ -110,7 +100,7 @@
     )(int_tiles.reshape(1, kt), integrals)
     everyone = lax.all_gather(packed, "grp")
     per = width // tile
-    step = 4
+    step = 16
     parts = pl.pallas_call(
         functools.partial(ladder_kernel, kt, tile),
         out_shape=jax.ShapeDtypeStruct((owners, rows + NOTE, width), jnp.int16),
@@ -123,18 +113,15 @@
         out_specs=pl.BlockSpec((step, rows + NOTE, width), lambda s: (s, 0, 0)),
         scratch_shapes=[
             pltpu.VMEM((rows, depth), jnp.bfloat16),
-            pltpu.VMEM((step, depth, width), jnp.bfloat16),
+            pltpu.VMEM((2, depth, width), jnp.bfloat16),
         ],
-        compiler_params=pltpu.CompilerParams(vmem_limit_bytes=32 * 2**20),
+        compiler_params=pltpu.CompilerParams(vmem_limit_bytes=20 * 2**20),
         name="ladder",
     )(amp_tiles, amplitudes, everyone)
-    return pl.pallas_call(
-        update_kernel,
-        out_shape=jax.ShapeDtypeStruct((rows, width), jnp.bfloat16),
-        in_specs=[VMEM, VMEM],
-        out_specs=VMEM,
-        name="update",
-    )(lax.all_to_all(parts, "mem", 0, 0), denominators)
+    parts = lax.all_to_all(parts, "mem", 0, 0)
+    scale = jnp.exp2(parts[:, rows : rows + 1].astype(jnp.float32) / -FINE)
+    ladder = jnp.sum(parts[:, :rows].astype(jnp.float32) * scale, axis=0)
+    return (ladder / denominators).astype(jnp.bfloat16)
 
 
 def solution(mesh):

time: 95.4 us -> 93.7 us (0.982)
  Pallas kernels: 9.44 us -> 6.55 us
  other arithmetic: 0 us -> 1.1 us
    pallas_call x1 -> x0, Pallas kernels: 2.21 us -> none  [on_device(): pl.pallas_call(update_kernel, out_shape=jax.ShapeDtypeStruct((rows, width...]
where the time goes in v5:
time: 93.7 us; the launch traced here: 93.5 us
  blocking collectives  85.8 us (92%)
  Pallas kernels  6.55 us (7%)
  other arithmetic  1.1 us (1%)
    all_gather x1, blocking collectives, on_device(): everyone = lax.all_gather(packed, 'grp')  60.8 us
    all_to_all x1, blocking collectives, on_device(): parts = lax.all_to_all(parts, 'mem', 0, 0)  25 us
    pallas_call x1, Pallas kernels, on_device(): pl.pallas_call(functools.partial(ladder_kernel, kt, tile), out_shape=jax....  4.81 us

profile of v5, /device:TPU:1, one launch (start us, length us, event | category | flops | bytes accessed | tf_op | source)
XLA Modules:
  0.0 93.5 jit_solution(451147693210924483)
XLA Ops:
  0.0 1.7 %pack.1 = s16[784,128]{1,0:T(8,128)(2,1)} custom-call(s32[1,8]{1,0:T(1,128)} %bitcast.7, bf16[1024,128]{1,0:T(8,128)(2,1)} %integrals_ref.1), custom_call_target="tpu_custom_call" | custom-call | tf_op jit(solution)/shard_map/pack/pallas_call | solution.py:94
  1.7 0.0 copy-start
  1.7 0.0 copy-start.1
  1.7 60.8 %all-gather.2 = s16[25088,128]{1,0:T(8,128)(2,1)S(1)} all-gather(s16[784,128]{1,0:T(8,128)(2,1)} %pack.1), channel_id=2, replica_groups=mesh['grp'=32,'mem'=16] {'grp'}, dimensions={0}, use_global_device_ids=true | all-gather | bytes 6623232 | tf_op jit(solution)/shard_map/all_gather | solution.py:101
  62.6 0.0 copy-done
  62.6 0.0 copy-done.1
  62.6 4.8 %ladder.1 = s16[16,144,256]{2,1,0:T(8,128)(2,1)S(1)} custom-call(s32[1,8]{1,0:T(1,128)S(1)} %copy-done.1, bf16[128,1024]{1,0:T(8,128)(2,1)S(1)} %copy-done, s16[32,784,128]{2,1,0:T(8,128)(2,1)S(1)} %bitcast.5), custom_call_target="tpu_custom_call" | custom-call | tf_op jit(solution)/shard_map/ladder/pallas_call | solution.py:104
  67.4 0.0 copy-start.2
  67.4 25.0 %all_to_all.5 = s16[16,144,256]{2,1,0:T(8,128)(2,1)S(1)} all-to-all(s16[16,144,256]{2,1,0:T(8,128)(2,1)S(1)} %ladder.1), channel_id=1, replica_groups=mesh['grp'=32,'mem'=16] {'mem'}, dimensions={0} | all-to-all | bytes 2359296 | tf_op jit(solution)/shard_map/all_to_all | solution.py:121
  92.4 0.4 multiply_reduce_fusion
  92.8 0.0 copy-done.2
  92.8 0.7 divide_convert_fusion
  (2 shorter events, 0.0 us)
Async XLA Ops:
  1.7 60.8 %copy-start = (bf16[128,1024]{1,0:T(8,128)(2,1)S(1)}, bf16[128,1024]{1,0:T(8,128)(2,1)}, u32[]{:S(2)}) copy-start(bf16[128,1024]{1,0:T(8,128)(2,1)} %amp_ref.1) | copy-start | bytes 786436
  1.7 60.8 %copy-start.1 = (s32[1,8]{1,0:T(1,128)S(1)}, s32[1,8]{1,0:T(1,128)}, u32[]{:S(2)}) copy-start(s32[1,8]{1,0:T(1,128)} %tiles_ref.1) | copy-start | bytes 100
  67.4 25.4 %copy-start.2 = (f32[128,256]{1,0:T(8,128)S(1)}, f32[128,256]{1,0:T(8,128)}, u32[]{:S(2)}) copy-start(f32[128,256]{1,0:T(8,128)} %param.9) | copy-start | bytes 393220

commit v6 on v5

--- a/solution.py
+++ b/solution.py
@@ -45,7 +45,7 @@
     out_ref[NZ * tile :] = note_of(notes, tile)
 
 
-def ladder_kernel(kt, tile, tiles_ref, amp_ref, packed_ref, out_ref, masked, full):
+def ladder_kernel(kt, tile, tiles_ref, amp_ref, packed_ref, out_ref, masked):
     groups = out_ref.shape[0]
     per = packed_ref.shape[0] // groups
     rows = amp_ref.shape[0]
@@ -60,6 +60,7 @@
             )
 
     for g in range(groups):
+        full = []
         for j in range(per):
             b = g * per + j
             note = packed_ref[b, NZ * tile :].astype(jnp.int32).astype(jnp.float32)
@@ -69,8 +70,9 @@
             place = [jnp.where(lag == o, scale, 0.0).astype(jnp.bfloat16) for o in lags]
             slots = []
             for i in range(NZ):
-                block = packed_ref[b, i * tile : (i + 1) * tile].astype(jnp.int32)
-                slots.append(block.astype(jnp.float32).astype(jnp.bfloat16))
+                block = packed_ref[b, i * tile : (i + 1) * tile]
+                slots.append(block.astype(jnp.bfloat16))
+            tiles = []
             for k in range(kt):
                 out = None
                 for o in lags:
@@ -78,8 +80,19 @@
                     if 0 <= i < NZ:
                         term = slots[i] * place[o][i : i + 1]
                         out = term if out is None else out + term
-                full[g % full.shape[0], k * tile : (k + 1) * tile, j * tile : (j + 1) * tile] = out
-        part = jnp.dot(masked[...], full[g % full.shape[0]], preferred_element_type=jnp.float32)
+                tiles.append(out)
+            full.append(tiles)
+        part = None
+        for k in range(0, kt, 2):
+            chunk = jnp.concatenate(
+                [jnp.concatenate([t[k], t[k + 1]], axis=0) for t in full], axis=1
+            )
+            term = jnp.dot(
+                masked[:, k * tile : (k + 2) * tile],
+                chunk,
+                preferred_element_type=jnp.float32,
+            )
+            part = term if part is None else part + term
         top = jnp.max(jnp.abs(part), axis=0, keepdims=True)
         shift = jnp.floor(FINE * (14.999 - jnp.log2(jnp.maximum(top, 1e-30))))
         out_ref[g, :rows] = to_int16(part * jnp.exp2(shift / FINE))
@@ -113,7 +126,6 @@
         out_specs=pl.BlockSpec((step, rows + NOTE, width), lambda s: (s, 0, 0)),
         scratch_shapes=[
             pltpu.VMEM((rows, depth), jnp.bfloat16),
-            pltpu.VMEM((2, depth, width), jnp.bfloat16),
         ],
         compiler_params=pltpu.CompilerParams(vmem_limit_bytes=20 * 2**20),
         name="ladder",

time: 93.7 us -> 92.4 us (0.986)
  Pallas kernels: 6.55 us -> 5.33 us
    pallas_call x1, Pallas kernels: 4.81 us -> 3.59 us  [on_device(): pl.pallas_call(functools.partial(ladder_kernel, kt, tile), out_shape=jax....]
where the time goes in v6:
time: 92.4 us; the launch traced here: 92.3 us
  blocking collectives  85.8 us (93%)
  Pallas kernels  5.33 us (6%)
  other arithmetic  1.1 us (1%)
    all_gather x1, blocking collectives, on_device(): everyone = lax.all_gather(packed, 'grp')  60.8 us
    all_to_all x1, blocking collectives, on_device(): parts = lax.all_to_all(parts, 'mem', 0, 0)  25 us
    pallas_call x1, Pallas kernels, on_device(): pl.pallas_call(functools.partial(ladder_kernel, kt, tile), out_shape=jax....  3.59 us

profile of v6, /device:TPU:1, one launch (start us, length us, event | category | flops | bytes accessed | tf_op | source)
XLA Modules:
  0.0 92.3 jit_solution(15343462591971912509)
XLA Ops:
  0.0 1.7 %pack.1 = s16[784,128]{1,0:T(8,128)(2,1)} custom-call(s32[1,8]{1,0:T(1,128)} %bitcast.7, bf16[1024,128]{1,0:T(8,128)(2,1)} %integrals_ref.1), custom_call_target="tpu_custom_call" | custom-call | tf_op jit(solution)/shard_map/pack/pallas_call | solution.py:107
  1.7 0.0 copy-start
  1.7 0.0 copy-start.1
  1.7 60.8 %all-gather.2 = s16[25088,128]{1,0:T(8,128)(2,1)S(1)} all-gather(s16[784,128]{1,0:T(8,128)(2,1)} %pack.1), channel_id=2, replica_groups=mesh['grp'=32,'mem'=16] {'grp'}, dimensions={0}, use_global_device_ids=true | all-gather | bytes 6623232 | tf_op jit(solution)/shard_map/all_gather | solution.py:114
  62.6 0.0 copy-done
  62.6 0.0 copy-done.1
  62.6 3.6 %ladder.1 = s16[16,144,256]{2,1,0:T(8,128)(2,1)S(1)} custom-call(s32[1,8]{1,0:T(1,128)S(1)} %copy-done.1, bf16[128,1024]{1,0:T(8,128)(2,1)S(1)} %copy-done, s16[32,784,128]{2,1,0:T(8,128)(2,1)S(1)} %bitcast.5), custom_call_target="tpu_custom_call" | custom-call | tf_op jit(solution)/shard_map/ladder/pallas_call | solution.py:117
  66.2 0.0 copy-start.2
  66.2 25.0 %all_to_all.5 = s16[16,144,256]{2,1,0:T(8,128)(2,1)S(1)} all-to-all(s16[16,144,256]{2,1,0:T(8,128)(2,1)S(1)} %ladder.1), channel_id=1, replica_groups=mesh['grp'=32,'mem'=16] {'mem'}, dimensions={0} | all-to-all | bytes 2359296 | tf_op jit(solution)/shard_map/all_to_all | solution.py:133
  91.2 0.4 multiply_reduce_fusion
  91.6 0.0 copy-done.2
  91.6 0.7 divide_convert_fusion
  (2 shorter events, 0.0 us)
Async XLA Ops:
  1.7 60.8 %copy-start = (bf16[128,1024]{1,0:T(8,128)(2,1)S(1)}, bf16[128,1024]{1,0:T(8,128)(2,1)}, u32[]{:S(2)}) copy-start(bf16[128,1024]{1,0:T(8,128)(2,1)} %amp_ref.1) | copy-start | bytes 786436
  1.7 60.8 %copy-start.1 = (s32[1,8]{1,0:T(1,128)S(1)}, s32[1,8]{1,0:T(1,128)}, u32[]{:S(2)}) copy-start(s32[1,8]{1,0:T(1,128)} %tiles_ref.1) | copy-start | bytes 100
  66.2 25.5 %copy-start.2 = (f32[128,256]{1,0:T(8,128)S(1)}, f32[128,256]{1,0:T(8,128)}, u32[]{:S(2)}) copy-start(f32[128,256]{1,0:T(8,128)} %param.9) | copy-start | bytes 393220

commit v7 on v6

--- a/solution.py
+++ b/solution.py
@@ -8,7 +8,7 @@
 from jax.sharding import PartitionSpec as P
 
 NZ = 6
-NOTE = 16
+NOTE = 8
 LAG = 256.0
 FINE = 8.0
 VMEM = pl.BlockSpec(memory_space=pltpu.VMEM)
@@ -94,7 +94,8 @@
             )
             part = term if part is None else part + term
         top = jnp.max(jnp.abs(part), axis=0, keepdims=True)
-        shift = jnp.floor(FINE * (14.999 - jnp.log2(jnp.maximum(top, 1e-30))))
+        shift = jnp.floor(FINE * (14.999 - jnp.log2(jnp.maximum(top, 1e-37))))
+        shift = jnp.minimum(shift, FINE * 125.0)
         out_ref[g, :rows] = to_int16(part * jnp.exp2(shift / FINE))
         out_ref[g, rows:] = note_of([shift], part.shape[1])
 

time: 92.4 us -> 91.1 us (0.986)
  blocking collectives: 85.8 us -> 84.5 us
    all_to_all x1, blocking collectives: 25 us -> 24 us  [on_device(): parts = lax.all_to_all(parts, 'mem', 0, 0)]
where the time goes in v7:
time: 91.1 us; the launch traced here: 91 us
  blocking collectives  84.5 us (93%)
  Pallas kernels  5.26 us (6%)
  other arithmetic  1.1 us (1%)
    all_gather x1, blocking collectives, on_device(): everyone = lax.all_gather(packed, 'grp')  60.5 us
    all_to_all x1, blocking collectives, on_device(): parts = lax.all_to_all(parts, 'mem', 0, 0)  24 us
    pallas_call x1, Pallas kernels, on_device(): pl.pallas_call(functools.partial(ladder_kernel, kt, tile), out_shape=jax....  3.52 us

profile of v7, /device:TPU:1, one launch (start us, length us, event | category | flops | bytes accessed | tf_op | source)
XLA Modules:
  0.0 91.0 jit_solution(16757581621522056831)
XLA Ops:
  0.0 1.7 %pack.1 = s16[776,128]{1,0:T(8,128)(2,1)} custom-call(s32[1,8]{1,0:T(1,128)} %bitcast.7, bf16[1024,128]{1,0:T(8,128)(2,1)} %integrals_ref.1), custom_call_target="tpu_custom_call" | custom-call | tf_op jit(solution)/shard_map/pack/pallas_call | solution.py:108
  1.7 0.0 copy-start
  1.7 0.0 copy-start.1
  1.7 60.5 %all-gather.2 = s16[24832,128]{1,0:T(8,128)(2,1)S(1)} all-gather(s16[776,128]{1,0:T(8,128)(2,1)} %pack.1), channel_id=2, replica_groups=mesh['grp'=32,'mem'=16] {'grp'}, dimensions={0}, use_global_device_ids=true | all-gather | bytes 6555648 | tf_op jit(solution)/shard_map/all_gather | solution.py:115
  62.3 0.0 copy-done
  62.3 0.0 copy-done.1
  62.3 3.5 %ladder.1 = s16[16,136,256]{2,1,0:T(8,128)(2,1)S(1)} custom-call(s32[1,8]{1,0:T(1,128)S(1)} %copy-done.1, bf16[128,1024]{1,0:T(8,128)(2,1)S(1)} %copy-done, s16[32,776,128]{2,1,0:T(8,128)(2,1)S(1)} %bitcast.5), custom_call_target="tpu_custom_call" | custom-call | tf_op jit(solution)/shard_map/ladder/pallas_call | solution.py:118
  65.8 0.0 copy-start.2
  65.8 24.0 %all_to_all.5 = s16[16,136,256]{2,1,0:T(8,128)(2,1)S(1)} all-to-all(s16[16,136,256]{2,1,0:T(8,128)(2,1)S(1)} %ladder.1), channel_id=1, replica_groups=mesh['grp'=32,'mem'=16] {'mem'}, dimensions={0} | all-to-all | bytes 2228224 | tf_op jit(solution)/shard_map/all_to_all | solution.py:134
  89.9 0.4 multiply_reduce_fusion
  90.3 0.0 copy-done.2
  90.3 0.7 divide_convert_fusion
  (2 shorter events, 0.0 us)
Async XLA Ops:
  1.7 60.6 %copy-start = (bf16[128,1024]{1,0:T(8,128)(2,1)S(1)}, bf16[128,1024]{1,0:T(8,128)(2,1)}, u32[]{:S(2)}) copy-start(bf16[128,1024]{1,0:T(8,128)(2,1)} %amp_ref.1) | copy-start | bytes 786436
  1.7 60.6 %copy-start.1 = (s32[1,8]{1,0:T(1,128)S(1)}, s32[1,8]{1,0:T(1,128)}, u32[]{:S(2)}) copy-start(s32[1,8]{1,0:T(1,128)} %tiles_ref.1) | copy-start | bytes 100
  65.8 24.5 %copy-start.2 = (f32[128,256]{1,0:T(8,128)S(1)}, f32[128,256]{1,0:T(8,128)}, u32[]{:S(2)}) copy-start(f32[128,256]{1,0:T(8,128)} %param.9) | copy-start | bytes 393220

commit v8 on v7

--- a/solution.py
+++ b/solution.py
@@ -66,21 +66,27 @@
             note = packed_ref[b, NZ * tile :].astype(jnp.int32).astype(jnp.float32)
             lag = jnp.floor(note / LAG)
             scale = jnp.exp2(LAG * lag - note)
-            lags = range(kt - NZ + 1)
-            place = [jnp.where(lag == o, scale, 0.0).astype(jnp.bfloat16) for o in lags]
-            slots = []
+            row = lax.broadcasted_iota(jnp.int32, note.shape, 0)
+            scale = jnp.where(row < NZ, scale, 0.0)
+            place = jnp.where(lag == 0, scale, 0.0)
+            for o in range(1, kt - NZ + 1):
+                place = place + pltpu.roll(jnp.where(lag == o, scale, 0.0), o, axis=0)
+            place = place.astype(jnp.bfloat16)
+            lag = lag.astype(jnp.bfloat16)
+            tiles = []
             for i in range(NZ):
                 block = packed_ref[b, i * tile : (i + 1) * tile]
-                slots.append(block.astype(jnp.bfloat16))
-            tiles = []
-            for k in range(kt):
-                out = None
-                for o in lags:
-                    i = k - o
-                    if 0 <= i < NZ:
-                        term = slots[i] * place[o][i : i + 1]
-                        out = term if out is None else out + term
-                tiles.append(out)
+                tiles.append(block.astype(jnp.bfloat16))
+            for o in range(1, kt - NZ + 1):
+                tiles = (
+                    tiles[:o]
+                    + [
+                        jnp.where(lag[i - o : i - o + 1] >= o, tiles[i - 1], tiles[i])
+                        for i in range(o, len(tiles))
+                    ]
+                    + tiles[-1:]
+                )
+            tiles = [tiles[k] * place[k : k + 1] for k in range(kt)]
             full.append(tiles)
         part = None
         for k in range(0, kt, 2):
@@ -98,6 +104,17 @@
         shift = jnp.minimum(shift, FINE * 125.0)
         out_ref[g, :rows] = to_int16(part * jnp.exp2(shift / FINE))
         out_ref[g, rows:] = note_of([shift], part.shape[1])
+
+
+def update_kernel(parts_ref, denominators_ref, out_ref):
+    rows = denominators_ref.shape[0]
+    total = None
+    for i in range(parts_ref.shape[0]):
+        note = parts_ref[i, rows:].astype(jnp.int32).astype(jnp.float32)
+        part = parts_ref[i, :rows].astype(jnp.int32).astype(jnp.float32)
+        part = part * jnp.exp2(note[:1] / -FINE)
+        total = part if total is None else total + part
+    out_ref[...] = (total / denominators_ref[...]).astype(out_ref.dtype)
 
 
 def on_device(amplitudes, amp_tiles, integrals, int_tiles, denominators):
@@ -132,9 +149,14 @@
         name="ladder",
     )(amp_tiles, amplitudes, everyone)
     parts = lax.all_to_all(parts, "mem", 0, 0)
-    scale = jnp.exp2(parts[:, rows : rows + 1].astype(jnp.float32) / -FINE)
-    ladder = jnp.sum(parts[:, :rows].astype(jnp.float32) * scale, axis=0)
-    return (ladder / denominators).astype(jnp.bfloat16)
+    return pl.pallas_call(
+        update_kernel,
+        out_shape=jax.ShapeDtypeStruct((rows, width), jnp.bfloat16),
+        in_specs=[VMEM, VMEM],
+        out_specs=VMEM,
+        compiler_params=pltpu.CompilerParams(vmem_limit_bytes=4 * 2**20),
+        name="update",
+    )(parts, denominators)
 
 
 def solution(mesh):

time: 91.1 us -> 90.7 us (level)
  other arithmetic: 1.1 us -> 0 us
    pallas_call x0 -> x1, Pallas kernels: none -> 0.93 us  [on_device(): pl.pallas_call(update_kernel, out_shape=jax.ShapeDtypeStruct((rows, width...]
where the time goes in v8:
time: 90.7 us; the launch traced here: 90.6 us
  blocking collectives  84.5 us (93%)
  Pallas kernels  6.07 us (7%)
    all_gather x1, blocking collectives, on_device(): everyone = lax.all_gather(packed, 'grp')  60.5 us
    all_to_all x1, blocking collectives, on_device(): parts = lax.all_to_all(parts, 'mem', 0, 0)  23.9 us
    pallas_call x1, Pallas kernels, on_device(): pl.pallas_call(functools.partial(ladder_kernel, kt, tile), out_shape=jax....  3.4 us

profile of v8, /device:TPU:1, one launch (start us, length us, event | category | flops | bytes accessed | tf_op | source)
XLA Modules:
  0.0 90.6 jit_solution(15310283730139481830)
XLA Ops:
  0.0 1.7 %pack.1 = s16[776,128]{1,0:T(8,128)(2,1)} custom-call(s32[1,8]{1,0:T(1,128)} %bitcast.3, bf16[1024,128]{1,0:T(8,128)(2,1)} %integrals_ref.1), custom_call_target="tpu_custom_call" | custom-call | tf_op jit(solution)/shard_map/pack/pallas_call | solution.py:125
  1.7 0.0 copy-start
  1.7 0.0 copy-start.2
  1.7 60.5 %all-gather.2 = s16[24832,128]{1,0:T(8,128)(2,1)S(1)} all-gather(s16[776,128]{1,0:T(8,128)(2,1)} %pack.1), channel_id=2, replica_groups=mesh['grp'=32,'mem'=16] {'grp'}, dimensions={0}, use_global_device_ids=true | all-gather | bytes 6555648 | tf_op jit(solution)/shard_map/all_gather | solution.py:132
  62.3 0.0 copy-done
  62.3 0.0 copy-done.2
  62.3 3.4 %ladder.1 = s16[16,136,256]{2,1,0:T(8,128)(2,1)S(1)} custom-call(s32[1,8]{1,0:T(1,128)S(1)} %copy-done.2, bf16[128,1024]{1,0:T(8,128)(2,1)S(1)} %copy-done, s16[32,776,128]{2,1,0:T(8,128)(2,1)S(1)} %bitcast.2), custom_call_target="tpu_custom_call" | custom-call | tf_op jit(solution)/shard_map/ladder/pallas_call | solution.py:135
  65.7 0.0 copy-start.1
  65.7 23.9 %all_to_all.5.parts_ref = s16[16,136,256]{2,1,0:T(8,128)(2,1)S(1)} all-to-all(s16[16,136,256]{2,1,0:T(8,128)(2,1)S(1)} %ladder.1), channel_id=1, replica_groups=mesh['grp'=32,'mem'=16] {'mem'}, dimensions={0} | all-to-all | bytes 2228224 | tf_op jit(solution)/shard_map/all_to_all | solution.py:151
  89.6 0.0 copy-done.1
  89.6 0.9 %update.1 = bf16[128,256]{1,0:T(8,128)(2,1)} custom-call(s16[16,136,256]{2,1,0:T(8,128)(2,1)S(1)} %all_to_all.5.parts_ref, f32[128,256]{1,0:T(8,128)S(1)} %copy-done.1), custom_call_target="tpu_custom_call" | custom-call | tf_op jit(solution)/shard_map/update/pallas_call | solution.py:152
Async XLA Ops:
  1.7 60.6 %copy-start = (bf16[128,1024]{1,0:T(8,128)(2,1)S(1)}, bf16[128,1024]{1,0:T(8,128)(2,1)}, u32[]{:S(2)}) copy-start(bf16[128,1024]{1,0:T(8,128)(2,1)} %amp_ref.1) | copy-start | bytes 786436
  1.7 60.6 %copy-start.2 = (s32[1,8]{1,0:T(1,128)S(1)}, s32[1,8]{1,0:T(1,128)}, u32[]{:S(2)}) copy-start(s32[1,8]{1,0:T(1,128)} %tiles_ref.1) | copy-start | bytes 100
  65.7 23.9 %copy-start.1 = (f32[128,256]{1,0:T(8,128)S(1)}, f32[128,256]{1,0:T(8,128)}, u32[]{:S(2)}) copy-start(f32[128,256]{1,0:T(8,128)} %denominators_ref.1) | copy-start | bytes 393220

commit v9 on v8

--- a/solution.py
+++ b/solution.py
@@ -88,17 +88,8 @@
                 )
             tiles = [tiles[k] * place[k : k + 1] for k in range(kt)]
             full.append(tiles)
-        part = None
-        for k in range(0, kt, 2):
-            chunk = jnp.concatenate(
-                [jnp.concatenate([t[k], t[k + 1]], axis=0) for t in full], axis=1
-            )
-            term = jnp.dot(
-                masked[:, k * tile : (k + 2) * tile],
-                chunk,
-                preferred_element_type=jnp.float32,
-            )
-            part = term if part is None else part + term
+        whole = jnp.concatenate([jnp.concatenate(t, axis=0) for t in full], axis=1)
+        part = jnp.dot(masked[...], whole, preferred_element_type=jnp.float32)
         top = jnp.max(jnp.abs(part), axis=0, keepdims=True)
         shift = jnp.floor(FINE * (14.999 - jnp.log2(jnp.maximum(top, 1e-37))))
         shift = jnp.minimum(shift, FINE * 125.0)

time: 90.7 us -> 90.7 us (level)
  no operation moved by 1% of the time
where the time goes in v9:
time: 90.7 us; the launch traced here: 90.5 us
  blocking collectives  84.5 us (93%)
  Pallas kernels  5.97 us (7%)
    all_gather x1, blocking collectives, on_device(): everyone = lax.all_gather(packed, 'grp')  60.5 us
    all_to_all x1, blocking collectives, on_device(): parts = lax.all_to_all(parts, 'mem', 0, 0)  24 us
    pallas_call x1, Pallas kernels, on_device(): pl.pallas_call(functools.partial(ladder_kernel, kt, tile), out_shape=jax....  3.3 us

profile of v9, /device:TPU:1, one launch (start us, length us, event | category | flops | bytes accessed | tf_op | source)
XLA Modules:
  0.0 90.5 jit_solution(6336114754775567553)
XLA Ops:
  0.0 1.7 %pack.1 = s16[776,128]{1,0:T(8,128)(2,1)} custom-call(s32[1,8]{1,0:T(1,128)} %bitcast.3, bf16[1024,128]{1,0:T(8,128)(2,1)} %integrals_ref.1), custom_call_target="tpu_custom_call" | custom-call | tf_op jit(solution)/shard_map/pack/pallas_call | solution.py:116
  1.7 0.0 copy-start
  1.7 0.0 copy-start.2
  1.7 60.5 %all-gather.2 = s16[24832,128]{1,0:T(8,128)(2,1)S(1)} all-gather(s16[776,128]{1,0:T(8,128)(2,1)} %pack.1), channel_id=2, replica_groups=mesh['grp'=32,'mem'=16] {'grp'}, dimensions={0}, use_global_device_ids=true | all-gather | bytes 6555648 | tf_op jit(solution)/shard_map/all_gather | solution.py:123
  62.3 0.0 copy-done
  62.3 0.0 copy-done.2
  62.3 3.3 %ladder.1 = s16[16,136,256]{2,1,0:T(8,128)(2,1)S(1)} custom-call(s32[1,8]{1,0:T(1,128)S(1)} %copy-done.2, bf16[128,1024]{1,0:T(8,128)(2,1)S(1)} %copy-done, s16[32,776,128]{2,1,0:T(8,128)(2,1)S(1)} %bitcast.2), custom_call_target="tpu_custom_call" | custom-call | tf_op jit(solution)/shard_map/ladder/pallas_call | solution.py:126
  65.6 0.0 copy-start.1
  65.6 24.0 %all_to_all.5.parts_ref = s16[16,136,256]{2,1,0:T(8,128)(2,1)S(1)} all-to-all(s16[16,136,256]{2,1,0:T(8,128)(2,1)S(1)} %ladder.1), channel_id=1, replica_groups=mesh['grp'=32,'mem'=16] {'mem'}, dimensions={0} | all-to-all | bytes 2228224 | tf_op jit(solution)/shard_map/all_to_all | solution.py:142
  89.6 0.0 copy-done.1
  89.6 0.9 %update.1 = bf16[128,256]{1,0:T(8,128)(2,1)} custom-call(s16[16,136,256]{2,1,0:T(8,128)(2,1)S(1)} %all_to_all.5.parts_ref, f32[128,256]{1,0:T(8,128)S(1)} %copy-done.1), custom_call_target="tpu_custom_call" | custom-call | tf_op jit(solution)/shard_map/update/pallas_call | solution.py:143
Async XLA Ops:
  1.7 60.6 %copy-start = (bf16[128,1024]{1,0:T(8,128)(2,1)S(1)}, bf16[128,1024]{1,0:T(8,128)(2,1)}, u32[]{:S(2)}) copy-start(bf16[128,1024]{1,0:T(8,128)(2,1)} %amp_ref.1) | copy-start | bytes 786436
  1.7 60.6 %copy-start.2 = (s32[1,8]{1,0:T(1,128)S(1)}, s32[1,8]{1,0:T(1,128)}, u32[]{:S(2)}) copy-start(s32[1,8]{1,0:T(1,128)} %tiles_ref.1) | copy-start | bytes 100
  65.6 24.0 %copy-start.1 = (f32[128,256]{1,0:T(8,128)S(1)}, f32[128,256]{1,0:T(8,128)}, u32[]{:S(2)}) copy-start(f32[128,256]{1,0:T(8,128)} %denominators_ref.1) | copy-start | bytes 393220

commit v10 on v8

--- a/solution.py
+++ b/solution.py
@@ -28,20 +28,25 @@
 
 
 def pack_kernel(kt, tile, tiles_ref, integrals_ref, out_ref):
-    ones = [tiles_ref[0, k] for k in range(kt)]
-    zeros = [sum(1 - ones[j] for j in range(k + 1)) for k in range(kt)]
+    ones = [
+        jnp.broadcast_to(tiles_ref[:, k : k + 1].astype(jnp.float32), (1, tile))
+        for k in range(kt)
+    ]
+    zeros = [sum(1.0 - ones[j] for j in range(k + 1)) for k in range(kt)]
     notes = []
     for i in range(NZ):
-        lag = 0
-        for o in range(kt - NZ):
-            lag = lag + (zeros[i + o] > o).astype(jnp.int32)
-        start = pl.multiple_of((i + lag) * tile, tile)
-        block = integrals_ref[pl.ds(start, tile), :].astype(jnp.float32)
+        block = integrals_ref[(kt - NZ + i) * tile : (kt - NZ + i + 1) * tile]
+        block = block.astype(jnp.float32)
+        lag = jnp.zeros((1, tile), jnp.float32)
+        for o in range(kt - NZ - 1, -1, -1):
+            nearer = integrals_ref[(i + o) * tile : (i + o + 1) * tile]
+            block = jnp.where(zeros[i + o] > o, block, nearer.astype(jnp.float32))
+            lag = lag + jnp.where(zeros[i + o] > o, 1.0, 0.0)
         top = jnp.max(jnp.abs(block), axis=0, keepdims=True)
         shift = jnp.floor(14.99 - jnp.log2(jnp.maximum(top, 1e-37)))
         shift = jnp.clip(shift, 0.0, 120.0)
         out_ref[i * tile : (i + 1) * tile] = to_int16(block * jnp.exp2(shift))
-        notes.append(shift + LAG * lag.astype(jnp.float32))
+        notes.append(shift + LAG * lag)
     out_ref[NZ * tile :] = note_of(notes, tile)
 
 
@@ -125,7 +130,7 @@
     packed = pl.pallas_call(
         functools.partial(pack_kernel, kt, tile),
         out_shape=jax.ShapeDtypeStruct((NZ * tile + NOTE, tile), jnp.int16),
-        in_specs=[SMEM, VMEM],
+        in_specs=[VMEM, VMEM],
         out_specs=VMEM,
         name="pack",
     )(int_tiles.reshape(1, kt), integrals)

time: 90.7 us -> 90.9 us (level)
  no operation moved by 1% of the time
where the time goes in v10:
time: 90.9 us; the launch traced here: 90.7 us
  blocking collectives  84.5 us (93%)
  Pallas kernels  6.17 us (7%)
    all_gather x1, blocking collectives, on_device(): everyone = lax.all_gather(packed, 'grp')  60.5 us
    all_to_all x1, blocking collectives, on_device(): parts = lax.all_to_all(parts, 'mem', 0, 0)  24 us
    pallas_call x1, Pallas kernels, on_device(): pl.pallas_call(functools.partial(ladder_kernel, kt, tile), out_shape=jax....  3.4 us
    pallas_call x1, Pallas kernels, on_device(): pl.pallas_call(functools.partial(pack_kernel, kt, tile), out_shape=jax.Sh...  1.83 us

profile of v10, /device:TPU:1, one launch (start us, length us, event | category | flops | bytes accessed | tf_op | source)
XLA Modules:
  0.0 90.7 jit_solution(17073989853359304486)
XLA Ops:
  0.0 1.8 %pack.1 = s16[776,128]{1,0:T(8,128)(2,1)} custom-call(s32[1,8]{1,0:T(1,128)} %bitcast.3, bf16[1024,128]{1,0:T(8,128)(2,1)} %integrals_ref.1), custom_call_target="tpu_custom_call" | custom-call | tf_op jit(solution)/shard_map/pack/pallas_call | solution.py:130
  1.8 0.0 copy-start
  1.8 0.0 copy-start.2
  1.8 60.5 %all-gather.2 = s16[24832,128]{1,0:T(8,128)(2,1)S(1)} all-gather(s16[776,128]{1,0:T(8,128)(2,1)} %pack.1), channel_id=2, replica_groups=mesh['grp'=32,'mem'=16] {'grp'}, dimensions={0}, use_global_device_ids=true | all-gather | bytes 6555648 | tf_op jit(solution)/shard_map/all_gather | solution.py:137
  62.4 0.0 copy-done
  62.4 0.0 copy-done.2
  62.4 3.4 %ladder.1 = s16[16,136,256]{2,1,0:T(8,128)(2,1)S(1)} custom-call(s32[1,8]{1,0:T(1,128)S(1)} %copy-done.2, bf16[128,1024]{1,0:T(8,128)(2,1)S(1)} %copy-done, s16[32,776,128]{2,1,0:T(8,128)(2,1)S(1)} %bitcast.2), custom_call_target="tpu_custom_call" | custom-call | tf_op jit(solution)/shard_map/ladder/pallas_call | solution.py:140
  65.8 0.0 copy-start.1
  65.8 24.0 %all_to_all.5.parts_ref = s16[16,136,256]{2,1,0:T(8,128)(2,1)S(1)} all-to-all(s16[16,136,256]{2,1,0:T(8,128)(2,1)S(1)} %ladder.1), channel_id=1, replica_groups=mesh['grp'=32,'mem'=16] {'mem'}, dimensions={0} | all-to-all | bytes 2228224 | tf_op jit(solution)/shard_map/all_to_all | solution.py:156
  89.8 0.0 copy-done.1
  89.8 0.9 %update.1 = bf16[128,256]{1,0:T(8,128)(2,1)} custom-call(s16[16,136,256]{2,1,0:T(8,128)(2,1)S(1)} %all_to_all.5.parts_ref, f32[128,256]{1,0:T(8,128)S(1)} %copy-done.1), custom_call_target="tpu_custom_call" | custom-call | tf_op jit(solution)/shard_map/update/pallas_call | solution.py:157
Async XLA Ops:
  1.8 60.6 %copy-start = (bf16[128,1024]{1,0:T(8,128)(2,1)S(1)}, bf16[128,1024]{1,0:T(8,128)(2,1)}, u32[]{:S(2)}) copy-start(bf16[128,1024]{1,0:T(8,128)(2,1)} %amp_ref.1) | copy-start | bytes 786436
  1.8 60.6 %copy-start.2 = (s32[1,8]{1,0:T(1,128)S(1)}, s32[1,8]{1,0:T(1,128)}, u32[]{:S(2)}) copy-start(s32[1,8]{1,0:T(1,128)} %tiles_ref.1) | copy-start | bytes 100
  65.8 24.0 %copy-start.1 = (f32[128,256]{1,0:T(8,128)S(1)}, f32[128,256]{1,0:T(8,128)}, u32[]{:S(2)}) copy-start(f32[128,256]{1,0:T(8,128)} %denominators_ref.1) | copy-start | bytes 393220
